TPU v7x, 128 devices: a whole 4x4x4 slice. The times are simulated.
128 devices in a mesh: row: 4 (over x), col: 16 (over z, y), depth: 2 (over core).
Axes of the slice: x: 4, y: 4, z: 4, core: 2. Of those that a mesh axis runs over, the one named last changes fastest.
Arguments:
- tokens: bfloat16 [1024, 6144], P(('depth', 'col'), 'row'), may hold values from -6 to 6
- w_in: bfloat16 [6144, 24576], P('row', 'col'), may hold values from -0.078125 to 0.078125
- w_out: bfloat16 [24576, 6144], P('col', 'row'), may hold values from -0.0390625 to 0.0390625
- cotangent: bfloat16 [1024, 6144], P(('depth', 'col'), 'row'), may hold values from -6 to 6
Outputs:
- output: bfloat16 [1024, 6144], P(('depth', 'col'), 'row')
- grad_tokens: bfloat16 [1024, 6144], P(('depth', 'col'), 'row')
- grad_w_in: bfloat16 [6144, 24576], P('row', ('col', 'depth'))
- grad_w_out: bfloat16 [24576, 6144], P(('col', 'depth'), 'row')
All inputs are finite; a program needn't handle non-finite values.
Results may differ from a plain program's by a relative error of at most 0.027.
Values may be sent and summed in bfloat16 or wider, within the bound.
A program may use at most 128 MiB of HBM per device.

v0:
```python
import jax
import jax.numpy as jnp
from jax import lax
from jax.sharding import PartitionSpec as P

root_coeff = 0.7978845608028654
cubic_coeff = 0.044715
contract_last = (((1,), (1,)), ((), ()))
contract_first = (((0,), (0,)), ((), ()))


def gelu_value(pre_act):
    inner = root_coeff * (pre_act + cubic_coeff * pre_act * pre_act * pre_act)
    return 0.5 * pre_act * (1.0 + jnp.tanh(inner))


def gelu_slope(pre_act):
    squared = pre_act * pre_act
    tangent = jnp.tanh(root_coeff * (pre_act + cubic_coeff * squared * pre_act))
    return 0.5 * (1.0 + tangent) + 0.5 * pre_act * (1.0 - tangent * tangent) * root_coeff * (
        1.0 + 3.0 * cubic_coeff * squared
    )


def body(tokens, w_in, w_out, cotangent):
    token_slab = lax.all_gather(tokens, "col", axis=0, tiled=True)
    pre_share = lax.psum_scatter(
        jnp.dot(token_slab, w_in, preferred_element_type=jnp.float32).astype(jnp.bfloat16),
        "row",
        scatter_dimension=0,
        tiled=True,
    ).astype(jnp.float32)
    hidden_share = gelu_value(pre_share).astype(jnp.bfloat16)
    hidden_slab = lax.all_gather(hidden_share, "row", axis=0, tiled=True)
    output = lax.psum_scatter(
        jnp.dot(hidden_slab, w_out, preferred_element_type=jnp.float32).astype(jnp.bfloat16),
        "col",
        scatter_dimension=0,
        tiled=True,
    )
    cotangent_slab = lax.all_gather(cotangent, "col", axis=0, tiled=True)
    rows_part = cotangent_slab
    grad_share = lax.psum_scatter(
        lax.dot_general(rows_part, w_out, contract_last, preferred_element_type=jnp.float32).astype(
            jnp.bfloat16
        ),
        "row",
        scatter_dimension=0,
        tiled=True,
    ).astype(jnp.float32)
    grad_pre = (grad_share * gelu_slope(pre_share)).astype(jnp.bfloat16)
    grad_slab = lax.all_gather(grad_pre, "row", axis=0, tiled=True)
    rows_part = grad_slab
    grad_tokens = lax.psum_scatter(
        lax.dot_general(rows_part, w_in, contract_last, preferred_element_type=jnp.float32).astype(
            jnp.bfloat16
        ),
        "col",
        scatter_dimension=0,
        tiled=True,
    )
    hidden_all = lax.all_to_all(hidden_slab, "depth", split_axis=1, concat_axis=0, tiled=True)
    grad_w_out = lax.dot_general(
        hidden_all,
        lax.all_gather(cotangent_slab, "depth", axis=0, tiled=True),
        contract_first,
        preferred_element_type=jnp.float32,
    )
    grad_all = lax.all_to_all(grad_slab, "depth", split_axis=1, concat_axis=0, tiled=True)
    grad_w_in = lax.dot_general(
        lax.all_gather(token_slab, "depth", axis=0, tiled=True),
        grad_all,
        contract_first,
        preferred_element_type=jnp.float32,
    )
    return (output, grad_tokens, grad_w_in.astype(jnp.bfloat16), grad_w_out.astype(jnp.bfloat16))


def solution(mesh):
    in_specs = (
        P(("depth", "col"), "row"),
        P("row", "col"),
        P("col", "row"),
        P(("depth", "col"), "row"),
    )
    out_specs = (
        P(("depth", "col"), "row"),
        P(("depth", "col"), "row"),
        P("row", ("col", "depth")),
        P(("col", "depth"), "row"),
    )
    return jax.shard_map(body, mesh=mesh, in_specs=in_specs, out_specs=out_specs, check_vma=False)
```

profile of v0, /device:TPU:0, one launch (start us, length us, event | category | flops | bytes accessed | tf_op | source)
XLA Modules:
  0.0 414.3 jit_solution(13600182011942562776)
XLA Ops:
  8.7 48.0 %all-gather.7.cloned.1.call-done = bf16[512,1536]{1,0:T(8,128)(2,1)} async-done(((bf16[32,1536]{1,0:T(8,128)(2,1)}), bf16[512,1536]{1,0:T(8,128)(2,1)}) %all-gather.7.cloned.1.call-update) | async-done | bytes 1572880 | tf_op jit(solution)/shard_map/all_gather | solution.py:26
  56.7 6.6 %convolution_convert_fusion.5 = bf16[512,1536]{1,0:T(8,128)(2,1)} fusion(bf16[512,1536]{1,0:T(8,128)(2,1)} %all-gather.7.cloned.1.call-done, bf16[1536,1536]{1,0:T(8,128)(2,1)} %param.5), kind=kOutput, calls=%fused_computation.6 | convolution fusion | flops 2416705536 | bytes 7864320 | tf_op jit(solution)/shard_map/dot_general | solution.py:28
  63.4 38.9 %all-gather.11.cloned.1.call-done = bf16[512,1536]{1,0:T(8,128)(2,1)} async-done(((bf16[32,1536]{1,0:T(8,128)(2,1)}), bf16[512,1536]{1,0:T(8,128)(2,1)}) %all-gather.11.cloned.1.call-update) | async-done | bytes 1572880 | tf_op jit(solution)/shard_map/all_gather | solution.py:41
  102.2 6.6 %convolution_convert_fusion.3 = bf16[512,1536]{1,0:T(8,128)(2,1)} fusion(bf16[512,1536]{1,0:T(8,128)(2,1)} %all-gather.11.cloned.1.call-done, bf16[1536,1536]{1,0:T(8,128)(2,1)} %param.6), kind=kOutput, calls=%fused_computation.4 | convolution fusion | flops 2416705536 | bytes 7864320 | tf_op jit(solution)/shard_map/dot_general | solution.py:44
  108.9 21.3 %reduce-scatter.5.cloned.1.call-done = bf16[128,1536]{1,0:T(8,128)(2,1)} async-done(((bf16[512,1536]{1,0:T(8,128)(2,1)}), bf16[128,1536]{1,0:T(8,128)(2,1)}) %reduce-scatter.5.cloned.1.call-update) | async-done | bytes 393232 | tf_op jit(solution)/shard_map/reduce_scatter | solution.py:27
  130.1 28.3 %reduce-scatter.9.cloned.1.call-done = bf16[128,1536]{1,0:T(8,128)(2,1)} async-done(((bf16[512,1536]{1,0:T(8,128)(2,1)}), bf16[128,1536]{1,0:T(8,128)(2,1)}) %reduce-scatter.9.cloned.1.call-update) | async-done | bytes 393232 | tf_op jit(solution)/shard_map/reduce_scatter | solution.py:43
  158.4 2.7 fusion.9
  163.3 24.3 %all-gather.9.cloned.1.call-done = bf16[512,1536]{1,0:T(8,128)(2,1)} async-done(((bf16[128,1536]{1,0:T(8,128)(2,1)}), bf16[512,1536]{1,0:T(8,128)(2,1)}) %all-gather.9.cloned.1.call-update) | async-done | bytes 1572880 | tf_op jit(solution)/shard_map/all_gather | solution.py:34
  187.6 6.6 %convolution_convert_fusion.4 = bf16[512,1536]{1,0:T(8,128)(2,1)} fusion(bf16[512,1536]{1,0:T(8,128)(2,1)} %all-gather.9.cloned.1.call-done, bf16[1536,1536]{1,0:T(8,128)(2,1)} %param.6), kind=kOutput, calls=%fused_computation.5 | convolution fusion | flops 2416705536 | bytes 7864320 | tf_op jit(solution)/shard_map/dot_general | solution.py:36
  194.3 22.0 %all-gather.13.cloned.1.call-done = bf16[512,1536]{1,0:T(8,128)(2,1)} async-done(((bf16[128,1536]{1,0:T(8,128)(2,1)}), bf16[512,1536]{1,0:T(8,128)(2,1)}) %all-gather.13.cloned.1.call-update) | async-done | bytes 1572880 | tf_op jit(solution)/shard_map/all_gather | solution.py:52
  216.3 6.6 %convolution_convert_fusion.2 = bf16[512,1536]{1,0:T(8,128)(2,1)} fusion(bf16[512,1536]{1,0:T(8,128)(2,1)} %all-gather.13.cloned.1.call-done, bf16[1536,1536]{1,0:T(8,128)(2,1)} %param.5), kind=kOutput, calls=%fused_computation.3 | convolution fusion | flops 2416705536 | bytes 7864320 | tf_op jit(solution)/shard_map/dot_general | solution.py:55
  223.0 1.4 copy-done
  224.3 1.2 copy.17
  225.6 3.8 all-to-all-start
  229.4 4.4 %all-gather.15.cloned.1.call-done = bf16[1024,1536]{1,0:T(8,128)(2,1)} async-done(((bf16[512,1536]{1,0:T(8,128)(2,1)}), bf16[1024,1536]{1,0:T(8,128)(2,1)}) %all-gather.15.cloned.1.call-update) | async-done | bytes 3145744 | tf_op jit(solution)/shard_map/all_gather | solution.py:71
  233.8 1.1 copy-done.1
  234.9 5.0 %fusion = bf16[1536,768]{0,1:T(8,128)(2,1)S(1)} fusion(bf16[1024,768]{1,0:T(8,128)(2,1)} %bitcast.30, bf16[1024,1536]{1,0:T(8,128)(2,1)} %all-gather.15.cloned.1.call-done), kind=kOutput, calls=%fused_computation.2 | convolution fusion | flops 2417098752 | bytes 7077888 | tf_op jit(solution)/shard_map/dot_general | solution.py:70
  239.9 2.4 copy.11
  242.3 2.7 copy.16
  245.0 3.8 all-to-all-start.1
  248.8 2.9 all-gather.17.cloned.1.call-done
  251.8 5.8 %convolution_convert_fusion = bf16[768,1536]{1,0:T(8,128)(2,1)} fusion(bf16[1024,768]{1,0:T(8,128)(2,1)S(1)} %bitcast.31, bf16[1024,1536]{1,0:T(8,128)(2,1)} %all-gather.17.cloned.1.call-done), kind=kOutput, calls=%fused_computation | convolution fusion | flops 2417098752 | bytes 7077888 | tf_op jit(solution)/shard_map/dot_general | solution.py:63
  257.6 73.2 %reduce-scatter.7.cloned.1.call-done = bf16[32,1536]{1,0:T(8,128)(2,1)} async-done(((bf16[512,1536]{1,0:T(8,128)(2,1)}), bf16[32,1536]{1,0:T(8,128)(2,1)}) %reduce-scatter.7.cloned.1.call-update) | async-done | bytes 98320 | tf_op jit(solution)/shard_map/reduce_scatter | solution.py:35
  330.8 76.6 %reduce-scatter.11.cloned.1.call-done = bf16[32,1536]{1,0:T(8,128)(2,1)} async-done(((bf16[512,1536]{1,0:T(8,128)(2,1)}), bf16[32,1536]{1,0:T(8,128)(2,1)}) %reduce-scatter.11.cloned.1.call-update) | async-done | bytes 98320 | tf_op jit(solution)/shard_map/reduce_scatter | solution.py:54
  (24 shorter events, 4.0 us)
Async XLA Ops:
  7.2 49.6 %all-gather.7.cloned.1.call-start = ((), (), s32[]{:S(2)}) async-start(), calls=%async_computation.6 | async-start | bytes 1671168 | tf_op jit(solution)/shard_map/all_gather | solution.py:26
  7.9 94.3 %all-gather.11.cloned.1.call-start = ((), (), s32[]{:S(2)}) async-start(), calls=%async_computation.10 | async-start | bytes 1671168 | tf_op jit(solution)/shard_map/all_gather | solution.py:41
  8.6 121.5 %reduce-scatter.5.cloned.1.call-start = ((), (), s32[]{:S(2)}) async-start(), calls=%async_computation.7 | async-start | bytes 1966080 | tf_op jit(solution)/shard_map/reduce_scatter | solution.py:27
  63.3 95.1 %reduce-scatter.9.cloned.1.call-start = ((), (), s32[]{:S(2)}) async-start(), calls=%async_computation.11 | async-start | bytes 1966080 | tf_op jit(solution)/shard_map/reduce_scatter | solution.py:43
  108.8 78.8 %all-gather.9.cloned.1.call-start = ((), (), s32[]{:S(2)}) async-start(), calls=%async_computation.8 | async-start | bytes 1966080 | tf_op jit(solution)/shard_map/all_gather | solution.py:34
  161.2 55.1 %all-gather.13.cloned.1.call-start = ((), (), s32[]{:S(2)}) async-start(), calls=%async_computation.12 | async-start | bytes 1966080 | tf_op jit(solution)/shard_map/all_gather | solution.py:52
  161.8 72.0 %all-gather.15.cloned.1.call-start = ((), (), s32[]{:S(2)}) async-start(), calls=%async_computation.14 | async-start | bytes 4718592 | tf_op jit(solution)/shard_map/all_gather | solution.py:71
  162.5 89.1 %all-gather.17.cloned.1.call-start = ((), (), s32[]{:S(2)}) async-start(), calls=%async_computation.15 | async-start | bytes 4718592 | tf_op jit(solution)/shard_map/all_gather | solution.py:65
  163.3 167.5 %reduce-scatter.7.cloned.1.call-start = ((), (), s32[]{:S(2)}) async-start(), calls=%async_computation.9 | async-start | bytes 1671168 | tf_op jit(solution)/shard_map/reduce_scatter | solution.py:35
  194.2 213.2 %reduce-scatter.11.cloned.1.call-start = ((), (), s32[]{:S(2)}) async-start(), calls=%async_computation.13 | async-start | bytes 1671168 | tf_op jit(solution)/shard_map/reduce_scatter | solution.py:54
  222.9 1.4 copy-start
  225.6 8.2 %all-to-all-start = ((bf16[512,2,768]{2,0,1:T(8,128)(2,1)}), bf16[512,2,768]{2,0,1:T(8,128)(2,1)S(1)}, u32[]{:S(2)}, u32[]{:S(2)}) async-start(bf16[512,2,768]{2,0,1:T(8,128)(2,1)} %bitcast.27), calls=%async_computation.4 | async-start | bytes 3145728 | tf_op jit(solution)/shard_map/all_to_all | solution.py:69
  233.8 1.1 copy-start.1
  245.0 6.8 %all-to-all-start.1 = ((bf16[512,2,768]{2,0,1:T(8,128)(2,1)}), bf16[512,2,768]{2,0,1:T(8,128)(2,1)S(1)}, u32[]{:S(2)}, u32[]{:S(2)}) async-start(bf16[512,2,768]{2,0,1:T(8,128)(2,1)} %bitcast.26), calls=%async_computation.5 | async-start | bytes 3145728 | tf_op jit(solution)/shard_map/all_to_all | solution.py:62
Sparse Core Ops, SparseCore 0:
  10.1 46.5 all-gather.6
  58.9 43.3 all-gather.10
  105.2 24.8 reduce-scatter.4
  133.0 25.4 reduce-scatter.8
  161.3 26.2 all-gather.8
  189.7 26.5 all-gather.12
  218.0 15.7 all-gather.14
  235.4 16.1 all-gather.16
  255.5 75.3 reduce-scatter.6
  334.4 72.9 reduce-scatter.10
where the time goes:
time: 415 us; the launch traced here: 414 us
  waiting for transfers between devices  343 us (83%)
  matrix products  37.1 us (9%)
  between operations  14.2 us (3%)
  local copies, waits for them, and re-layouts  8.86 us (2%)
  starting transfers between devices  7.96 us (2%)
    reduce_scatter x1, waiting for transfers between devices, body(): lax.psum_scatter(lax.dot_general(rows_part, w_in, contract_last, preferre...  76.6 us
    reduce_scatter x1, waiting for transfers between devices, body(): lax.psum_scatter(jnp.dot(hidden_slab, w_out, preferred_element_type=jnp.f...  73.2 us
    all_gather x1, waiting for transfers between devices, body(): token_slab = lax.all_gather(tokens, 'col', axis=0, tiled=True)  48 us
    all_gather x1, waiting for transfers between devices, body(): cotangent_slab = lax.all_gather(cotangent, 'col', axis=0, tiled=True)  38.9 us
    reduce_scatter x1, waiting for transfers between devices, body(): lax.psum_scatter(lax.dot_general(rows_part, w_out, contract_last, preferr...  28.3 us
    all_gather x1, waiting for transfers between devices, body(): hidden_slab = lax.all_gather(hidden_share, 'row', axis=0, tiled=True)  24.3 us
    all_gather x1, waiting for transfers between devices, body(): grad_slab = lax.all_gather(grad_pre, 'row', axis=0, tiled=True)  22 us
    reduce_scatter x1, waiting for transfers between devices, body(): lax.psum_scatter(jnp.dot(token_slab, w_in, preferred_element_type=jnp.flo...  21.3 us
  transfers between devices with their start and end apart: 12, of which 11 were waited for; matrix products, arithmetic and copies ran while one was open for 10% of the time, Pallas kernels for 0%

commit v1 on v0

v1 whole, which is shorter than its diff:
```python
import jax
import jax.numpy as jnp
from jax import lax
from jax.experimental import pallas as pl
from jax.experimental.pallas import tpu as pltpu
from jax.sharding import PartitionSpec as P

MESH = pl.DeviceIdType.MESH
root_coeff = 0.7978845608028654
cubic_coeff = 0.044715
contract_last = (((1,), (1,)), ((), ()))
contract_first = (((0,), (0,)), ((), ()))
f32 = jnp.float32
bf16 = jnp.bfloat16
FWD, BWD = 0, 1
STEP = (0, 1, 3, 2)
TILE = 512


def gelu_value(pre_act):
    inner = root_coeff * (pre_act + cubic_coeff * pre_act * pre_act * pre_act)
    return 0.5 * pre_act * (1.0 + jnp.tanh(inner))


def gelu_slope(pre_act):
    squared = pre_act * pre_act
    tangent = jnp.tanh(root_coeff * (pre_act + cubic_coeff * squared * pre_act))
    return 0.5 * (1.0 + tangent) + 0.5 * pre_act * (1.0 - tangent * tangent) * root_coeff * (
        1.0 + 3.0 * cubic_coeff * squared
    )


def mod4(value):
    return lax.rem(value + 8, 4)


def kernel(
    tokens, w_in_hbm, w_out_hbm, cotangent,
    output, grad_tokens, grad_w_in, grad_w_out,
    w_in, w_out, slabs, other, share, passing, final, pre, act, act_other,
    share2, phase1, row_sum, phase2, out_buf, gw_in, gw_out,
    load_sem, gather_s, gather_r, scat_s, scat_r, spread_s, spread_r,
    depth_s, depth_r, col_s, col_r, store_sem,
):
    x = lax.axis_index("row")
    c = lax.axis_index("col")
    d = lax.axis_index("depth")
    z, y = c // 4, lax.rem(c, 4)
    left, right = mod4(x - 1), mod4(x + 1)
    axis_me = (z, y)

    def at_x(value):
        return {"row": value, "col": c, "depth": d}

    def at_z(value):
        return {"row": x, "col": value * 4 + y, "depth": d}

    def at_y(value):
        return {"row": x, "col": z * 4 + value, "depth": d}

    sibling = {"row": x, "col": c, "depth": 1 - d}

    def remote(src, dst, send, recv, device):
        return pltpu.make_async_remote_copy(
            src_ref=src, dst_ref=dst, send_sem=send, recv_sem=recv, device_id=device, device_id_type=MESH
        )

    sent = []

    def push(src, dst, send, recv, device):
        copy = remote(src, dst, send, recv, device)
        copy.start()
        sent.append(copy)

    def arrived(ref, send, recv):
        remote(ref, ref, send, recv, sibling).wait_recv()

    load_tok = pltpu.make_async_copy(tokens, slabs.at[FWD, z, y], load_sem.at[0])
    load_cot = pltpu.make_async_copy(cotangent, slabs.at[BWD, z, y], load_sem.at[1])
    load_in = pltpu.make_async_copy(w_in_hbm, w_in, load_sem.at[2])
    load_out = pltpu.make_async_copy(w_out_hbm, w_out, load_sem.at[3])
    for load in (load_tok, load_cot, load_in, load_out):
        load.start()

    barrier = pltpu.get_barrier_semaphore()
    peers = [at_x(left), at_x(right), sibling]
    for step in (1, 2, 3):
        peers += [at_z(mod4(z + step)), at_y(mod4(y + step))]
    for peer in peers:
        pl.semaphore_signal(barrier, inc=1, device_id=peer, device_id_type=MESH)
    pl.semaphore_wait(barrier, len(peers))

    def place(direction, k):
        return mod4(axis_me[direction] + STEP[k])

    def chunk(ref, direction, at):
        return ref.at[at] if direction == FWD else ref.at[:, at]

    def near(direction, value):
        return at_y(value) if direction == FWD else at_z(value)

    def far(direction, value):
        return at_z(value) if direction == FWD else at_y(value)

    def near_me(direction):
        return axis_me[1 - direction]

    def far_me(direction):
        return axis_me[direction]

    for direction, load in ((FWD, load_tok), (BWD, load_cot)):
        load.wait()
        own = slabs.at[direction, z, y]
        for j in (1, 2, 3):
            push(own, own, gather_s.at[direction, 0, j - 1], gather_r.at[direction, 0, j - 1],
                 near(direction, mod4(near_me(direction) + STEP[j])))

    def gather(direction, k):
        at = place(direction, k)
        blocks = chunk(slabs.at[direction], direction, at)
        if k == 0:
            for j in (1, 2, 3):
                source = mod4(near_me(direction) - STEP[j])
                block = blocks.at[source]
                arrived(block, gather_s.at[direction, 0, j - 1], gather_r.at[direction, 0, j - 1])
            for j in (1, 2, 3):
                push(blocks, blocks, gather_s.at[direction, 1, j - 1], gather_r.at[direction, 1, j - 1],
                     far(direction, mod4(far_me(direction) + STEP[j])))
        else:
            j = {1: 2, 2: 1, 3: 3}[k]
            arrived(blocks, gather_s.at[direction, 1, j - 1], gather_r.at[direction, 1, j - 1])
        push(blocks, chunk(other.at[direction], direction, at),
             depth_s.at[direction, k], depth_r.at[direction, k], sibling)

    def first_matmul(direction, k):
        at = place(direction, k)
        lhs = chunk(slabs.at[direction], direction, at)

        def tile(i, carry):
            cols = pl.ds(pl.multiple_of(i * TILE, TILE), TILE)
            rows = lhs[...].reshape(128, 1536)
            if direction == FWD:
                product = jnp.dot(rows, w_in[:, cols], preferred_element_type=f32)
            else:
                product = lax.dot_general(rows, w_out[cols, :], contract_last, preferred_element_type=f32)
            share[direction, at, :, :, cols] = product.astype(bf16).reshape(4, 32, TILE)
            return carry

        lax.fori_loop(0, 1536 // TILE, tile, 0)
        piece = lambda owner: share.at[direction, at, mod4(owner - at)]
        low, high = pl.ds(0, 16), pl.ds(16, 16)
        s = lambda n: scat_s.at[direction, k, n]
        r = lambda n: scat_r.at[direction, k, n]
        far_piece = piece(x + 2)
        push(far_piece.at[low], passing.at[direction, k, 0], s(0), r(0), at_x(right))
        push(far_piece.at[high], passing.at[direction, k, 1], s(1), r(1), at_x(left))
        push(piece(x + 1).at[high], final.at[direction, k, 0, high], s(2), r(2), at_x(right))
        push(piece(x - 1).at[low], final.at[direction, k, 1, low], s(3), r(3), at_x(left))

    def pass_on(direction, k):
        at = place(direction, k)
        low, high = pl.ds(0, 16), pl.ds(16, 16)
        for side, part, owner, n, m, to in ((0, low, x + 1, 0, 4, right), (1, high, x - 1, 1, 5, left)):
            arrived(passing.at[direction, k, side], scat_s.at[direction, k, n], scat_r.at[direction, k, n])
            mine = share.at[direction, at, mod4(owner - at)]
            total = mine[part].astype(f32) + passing[direction, k, side].astype(f32)
            mine[part] = total.astype(bf16)
            push(mine.at[part], final.at[direction, k, side, part],
                 scat_s.at[direction, k, m], scat_r.at[direction, k, m], at_x(to))

    def activate(direction, k):
        at = place(direction, k)
        low, high = pl.ds(0, 16), pl.ds(16, 16)
        for side, part, n in ((0, high, 2), (1, low, 3), (0, low, 4), (1, high, 5)):
            arrived(final.at[direction, k, side, part], scat_s.at[direction, k, n], scat_r.at[direction, k, n])
        block = mod4(x - at)
        mine = share.at[direction, at, block]
        place_z = at if direction == FWD else block
        place_y = block if direction == FWD else at
        result = act.at[direction, place_z, place_y]

        def rows(i, carry):
            part = pl.ds(pl.multiple_of(i * 16, 16), 16)
            total = mine[part].astype(f32)
            total = total + final[direction, k, 0, part].astype(f32)
            total = total + final[direction, k, 1, part].astype(f32)
            if direction == FWD:
                pre[place_z, part] = total
                result[part] = gelu_value(total).astype(bf16)
            else:
                result[part] = (total * gelu_slope(pre[place_z, part])).astype(bf16)
            return carry

        lax.fori_loop(0, 2, rows, 0)
        for n, to in ((0, right), (1, left)):
            push(result, result, spread_s.at[direction, k, n], spread_r.at[direction, k, n], at_x(to))

    def block_of(direction, at, owner):
        block = mod4(owner - at)
        return act.at[direction, at, block] if direction == FWD else act.at[direction, block, at]

    def forward_on(direction, k):
        at = place(direction, k)
        low, high = pl.ds(0, 16), pl.ds(16, 16)
        for source, part, n, to in ((x - 1, low, 0, right), (x + 1, high, 1, left)):
            block = block_of(direction, at, source)
            arrived(block, spread_s.at[direction, k, n], spread_r.at[direction, k, n])
            push(block.at[part], block.at[part], spread_s.at[direction, k, n + 2],
                 spread_r.at[direction, k, n + 2], at_x(to))

    def second_matmul(direction, k):
        at = place(direction, k)
        block = block_of(direction, at, x + 2)
        for n, part in ((2, pl.ds(0, 16)), (3, pl.ds(16, 16))):
            arrived(block.at[part], spread_s.at[direction, k, n], spread_r.at[direction, k, n])
        lhs = chunk(act.at[direction], direction, at)
        half = pl.ds(pl.multiple_of((1 - d) * 768, 128), 768)
        push(lhs.at[:, :, half], chunk(act_other.at[direction], direction, at),
             depth_s.at[direction, 4 + k], depth_r.at[direction, 4 + k], sibling)

        def tile(i, carry):
            cols = pl.ds(pl.multiple_of(i * TILE, TILE), TILE)
            rows = lhs[...].reshape(128, 1536)
            if direction == FWD:
                product = jnp.dot(rows, w_out[:, cols], preferred_element_type=f32)
            else:
                product = lax.dot_general(rows, w_in[cols, :], contract_last, preferred_element_type=f32)
            share2[direction, at, :, :, cols] = product.astype(bf16).reshape(4, 32, TILE)
            return carry

        lax.fori_loop(0, 1536 // TILE, tile, 0)
        if k:
            push(share2.at[direction, at], phase1.at[direction, k - 1],
                 col_s.at[direction, 0, k - 1], col_r.at[direction, 0, k - 1], far(direction, at))

    def sum_far(direction):
        at = place(direction, 0)
        for j in (1, 2, 3):
            arrived(phase1.at[direction, j - 1], col_s.at[direction, 0, j - 1], col_r.at[direction, 0, j - 1])

        def block(i, carry):
            total = share2[direction, at, i].astype(f32)
            for j in (0, 1, 2):
                total = total + phase1[direction, j, i].astype(f32)
            row_sum[direction, i] = total.astype(bf16)
            return carry

        lax.fori_loop(0, 4, block, 0)
        for j in (1, 2, 3):
            to = mod4(near_me(direction) + STEP[j])
            push(row_sum.at[direction, to], phase2.at[direction, j - 1],
                 col_s.at[direction, 1, j - 1], col_r.at[direction, 1, j - 1], near(direction, to))

    stores = []

    def sum_near(direction):
        for j in (1, 2, 3):
            arrived(phase2.at[direction, j - 1], col_s.at[direction, 1, j - 1], col_r.at[direction, 1, j - 1])
        total = row_sum[direction, near_me(direction)].astype(f32)
        for j in (0, 1, 2):
            total = total + phase2[direction, j].astype(f32)
        out_buf[direction] = total.astype(bf16)
        store = pltpu.make_async_copy(out_buf.at[direction], (output, grad_tokens)[direction], store_sem.at[direction])
        store.start()
        stores.append(store)

    def weight_grad(which):
        for k in range(4):
            arrived(chunk(other.at[1 - which], 1 - which, place(1 - which, k)),
                    depth_s.at[1 - which, k], depth_r.at[1 - which, k])
            arrived(chunk(act_other.at[which], which, place(which, k)),
                    depth_s.at[which, 4 + k], depth_r.at[which, 4 + k])
        width = 768 if which == FWD else 1536
        half = pl.multiple_of(d * 768, 128)
        result = gw_out if which == FWD else gw_in
        target = grad_w_out if which == FWD else grad_w_in

        def tile(i, carry):
            start = pl.multiple_of(i * 256, 256)
            rows = pl.ds(start, 256)
            if which == FWD:
                lhs = act[FWD, :, :, :, pl.ds(half + start, 256)].reshape(512, 256)
                rhs = slabs[BWD].reshape(512, 1536)
                lhs_other = act_other[FWD, :, :, :, rows].reshape(512, 256)
                rhs_other = other[BWD].reshape(512, 1536)
            else:
                lhs = slabs[FWD, :, :, :, rows].reshape(512, 256)
                rhs = act[BWD, :, :, :, pl.ds(half, 768)].reshape(512, 768)
                lhs_other = other[FWD, :, :, :, rows].reshape(512, 256)
                rhs_other = act_other[BWD].reshape(512, 768)
            product = lax.dot_general(lhs, rhs, contract_first, preferred_element_type=f32)
            product = product + lax.dot_general(lhs_other, rhs_other, contract_first, preferred_element_type=f32)
            result[rows] = product.astype(bf16)
            return carry

        lax.fori_loop(0, width // 256, tile, 0)
        store = pltpu.make_async_copy(result, target, store_sem.at[2 + which])
        store.start()
        stores.append(store)

    F, B = FWD, BWD
    gather(F, 0)
    gather(B, 0)
    load_in.wait()
    first_matmul(F, 0)
    load_out.wait()
    first_matmul(B, 0)
    pass_on(F, 0)
    gather(F, 1)
    first_matmul(F, 1)
    pass_on(B, 0)
    activate(F, 0)
    gather(B, 1)
    first_matmul(B, 1)
    pass_on(F, 1)
    forward_on(F, 0)
    gather(F, 2)
    first_matmul(F, 2)
    pass_on(B, 1)
    activate(F, 1)
    gather(B, 2)
    first_matmul(B, 2)
    pass_on(F, 2)
    forward_on(F, 1)
    second_matmul(F, 0)
    gather(F, 3)
    first_matmul(F, 3)
    pass_on(B, 2)
    activate(F, 2)
    gather(B, 3)
    first_matmul(B, 3)
    pass_on(F, 3)
    forward_on(F, 2)
    second_matmul(F, 1)
    activate(F, 3)
    pass_on(B, 3)
    activate(B, 1)
    forward_on(F, 3)
    second_matmul(F, 2)
    activate(B, 2)
    forward_on(B, 1)
    second_matmul(F, 3)
    activate(B, 3)
    forward_on(B, 2)
    second_matmul(B, 1)
    activate(B, 0)
    sum_far(F)
    forward_on(B, 3)
    second_matmul(B, 2)
    weight_grad(FWD)
    forward_on(B, 0)
    second_matmul(B, 3)
    sum_near(F)
    second_matmul(B, 0)
    sum_far(B)
    weight_grad(BWD)
    sum_near(B)
    for copy in sent:
        copy.wait_send()
    for store in stores:
        store.wait()


def body(tokens, w_in, w_out, cotangent):
    anywhere = pl.BlockSpec(memory_space=pl.ANY)
    dma = pltpu.SemaphoreType.DMA
    vmem = pltpu.VMEM
    return pl.pallas_call(
        kernel,
        out_shape=(
            jax.ShapeDtypeStruct((32, 1536), bf16),
            jax.ShapeDtypeStruct((32, 1536), bf16),
            jax.ShapeDtypeStruct((1536, 768), bf16),
            jax.ShapeDtypeStruct((768, 1536), bf16),
        ),
        in_specs=[anywhere] * 4,
        out_specs=(anywhere,) * 4,
        scratch_shapes=[
            vmem((1536, 1536), bf16),
            vmem((1536, 1536), bf16),
            vmem((2, 4, 4, 32, 1536), bf16),
            vmem((2, 4, 4, 32, 1536), bf16),
            vmem((2, 4, 4, 32, 1536), bf16),
            vmem((2, 4, 2, 16, 1536), bf16),
            vmem((2, 4, 2, 32, 1536), bf16),
            vmem((4, 32, 1536), f32),
            vmem((2, 4, 4, 32, 1536), bf16),
            vmem((2, 4, 4, 32, 768), bf16),
            vmem((2, 4, 4, 32, 1536), bf16),
            vmem((2, 3, 4, 32, 1536), bf16),
            vmem((2, 4, 32, 1536), bf16),
            vmem((2, 3, 32, 1536), bf16),
            vmem((2, 32, 1536), bf16),
            vmem((1536, 768), bf16),
            vmem((768, 1536), bf16),
            dma((4,)),
            dma((2, 2, 3)), dma((2, 2, 3)),
            dma((2, 4, 6)), dma((2, 4, 6)),
            dma((2, 4, 4)), dma((2, 4, 4)),
            dma((2, 8)), dma((2, 8)),
            dma((2, 2, 3)), dma((2, 2, 3)),
            dma((4,)),
        ],
        compiler_params=pltpu.CompilerParams(
            collective_id=1, has_side_effects=True, vmem_limit_bytes=60 * 2**20
        ),
        cost_estimate=pl.CostEstimate(flops=14_500_000_000, bytes_accessed=15_000_000, transcendentals=0),
        name="ffn_block",
    )(tokens, w_in, w_out, cotangent)


def solution(mesh):
    in_specs = (
        P(("depth", "col"), "row"),
        P("row", "col"),
        P("col", "row"),
        P(("depth", "col"), "row"),
    )
    out_specs = (
        P(("depth", "col"), "row"),
        P(("depth", "col"), "row"),
        P("row", ("col", "depth")),
        P(("col", "depth"), "row"),
    )
    return jax.shard_map(body, mesh=mesh, in_specs=in_specs, out_specs=out_specs, check_vma=False)
```

time: 415 us -> 105 us (0.25)
  waiting for transfers between devices: 343 us -> 0 us
  Pallas kernels: 0 us -> 96.5 us
  matrix products: 37.1 us -> 0 us
  between operations: 14.2 us -> 0.64 us
  starting transfers between devices: 7.96 us -> 0 us
    reduce_scatter x4 -> x0, waiting for transfers between devices: 199 us -> none  [the longest x1 76.6 us: body(): lax.psum_scatter(lax.dot_general(rows_part, w_in, contract_last, preferre...]
    all_gather x6 -> x0, waiting for transfers between devices: 140 us -> none  [the longest x1 48 us: body(): token_slab = lax.all_gather(tokens, 'col', axis=0, tiled=True)]
    pallas_call x0 -> x1, Pallas kernels: none -> 96.5 us  [body(): pl.pallas_call(kernel, out_shape=(jax.ShapeDtypeStruct((32, 1536), bf16),...]
    dot_general x6 -> x0, matrix products: 37.1 us -> none  [the longest x1 6.62 us: body(): lax.dot_general(rows_part, w_in, contract_last, preferred_element_type=jn...]
    all_to_all x2 -> x0, starting transfers between devices: 7.57 us -> none  [the longest x1 3.79 us: body(): lax.all_to_all(hidden_slab, 'depth', split_axis=1, concat_axis=0, tiled=T...]
  transfers between devices with their start and end apart: 12 -> 0, of which waited for: 11 -> 0; matrix products, arithmetic and copies ran while one was open for 10% -> 0% of each run, Pallas kernels for 0% -> 0%
where the time goes in v1:
time: 105 us
  Pallas kernels  96.5 us (92%)
  local copies, waits for them, and re-layouts  7.86 us (7%)
    pallas_call x1, Pallas kernels, body(): pl.pallas_call(kernel, out_shape=(jax.ShapeDtypeStruct((32, 1536), bf16),...  96.5 us
    unnamed x6, local copies, waits for them, and re-layouts  7.86 us

profile of v1, /device:TPU:0, one launch (start us, length us, event | category | flops | bytes accessed | tf_op | source)
XLA Modules:
  0.0 105.0 jit_solution(13106227705879052543)
XLA Ops:
  0.6 96.5 %ffn_block.1 = (bf16[32,1536]{1,0:T(8,128)(2,1)}, bf16[32,1536]{1,0:T(8,128)(2,1)}, bf16[1536,768]{1,0:T(8,128)(2,1)}, bf16[768,1536]{1,0:T(8,128)(2,1)}) custom-call(bf16[32,1536]{1,0:T(8,128)(2,1)} %tokens.1, bf16[1536,1536]{1,0:T(8,128)(2,1)} %w_in_hbm.1, bf16[1536,1536]{1,0:T(8,128)(2,1)} %w_out_hbm.1, bf16[32,1536]{1,0:T(8,128)(2,1)} %cotangent.1), custom_call_target="tpu_custom_call" | custom-call | flops 14499999744 | bytes 15000000 | tf_op jit(solution)/shard_map/ffn_block/pallas_call | solution.py:368
  97.1 1.5 %copy.12 = bf16[32,1536]{1,0:T(8,128)(2,1)} copy(bf16[32,1536]{1,0:T(8,128)(2,1)} %get-tuple-element.8) | data formatting | bytes 196608
  98.7 1.5 %copy.13 = bf16[32,1536]{1,0:T(8,128)(2,1)} copy(bf16[32,1536]{1,0:T(8,128)(2,1)} %get-tuple-element.9) | data formatting | bytes 196608
  100.2 0.0 copy-start
  100.2 3.4 %copy.14 = bf16[1536,768]{1,0:T(8,128)(2,1)} copy(bf16[1536,768]{1,0:T(8,128)(2,1)} %get-tuple-element.10) | data formatting | bytes 4718592
  103.6 0.0 copy-done
  103.6 1.4 %copy.15 = bf16[768,1536]{1,0:T(8,128)(2,1)} copy(bf16[768,1536]{1,0:T(8,128)(2,1)S(1)} %copy-done) | data formatting | bytes 4718592
Async XLA Ops:
  100.2 3.4 %copy-start = (bf16[768,1536]{1,0:T(8,128)(2,1)S(1)}, bf16[768,1536]{1,0:T(8,128)(2,1)}, u32[]{:S(2)}) copy-start(bf16[768,1536]{1,0:T(8,128)(2,1)} %get-tuple-element.11) | copy-start | bytes 7077892

commit v2 on v1

v2 whole, which is shorter than its diff:
```python
import jax
import jax.numpy as jnp
from jax import lax
from jax.experimental import pallas as pl
from jax.experimental.pallas import tpu as pltpu
from jax.sharding import PartitionSpec as P

MESH = pl.DeviceIdType.MESH
root_coeff = 0.7978845608028654
cubic_coeff = 0.044715
contract_last = (((1,), (1,)), ((), ()))
contract_first = (((0,), (0,)), ((), ()))
f32 = jnp.float32
bf16 = jnp.bfloat16
FWD, BWD = 0, 1
STEP = (0, 1, 3, 2)
TILE = 512


def gelu_value(pre_act):
    inner = root_coeff * (pre_act + cubic_coeff * pre_act * pre_act * pre_act)
    return 0.5 * pre_act * (1.0 + jnp.tanh(inner))


def gelu_slope(pre_act):
    squared = pre_act * pre_act
    tangent = jnp.tanh(root_coeff * (pre_act + cubic_coeff * squared * pre_act))
    return 0.5 * (1.0 + tangent) + 0.5 * pre_act * (1.0 - tangent * tangent) * root_coeff * (
        1.0 + 3.0 * cubic_coeff * squared
    )


def mod4(value):
    return lax.rem(value + 8, 4)


def kernel(
    tokens, w_in_hbm, w_out_hbm, cotangent,
    output, grad_tokens, grad_w_in, grad_w_out,
    w_in, w_out, slabs, other, share, passing, final, pre, act, act_other,
    share2, passing1, final1, row_sum, passing2, final2, out_buf, gw_in, gw_out,
    load_sem, gather_s, gather_r, scat_s, scat_r, spread_s, spread_r,
    depth_s, depth_r, col_s, col_r, store_sem,
):
    x = lax.axis_index("row")
    c = lax.axis_index("col")
    d = lax.axis_index("depth")
    z, y = c // 4, lax.rem(c, 4)
    left, right = mod4(x - 1), mod4(x + 1)
    axis_me = (z, y)

    def at_x(value):
        return {"row": value, "col": c, "depth": d}

    def at_z(value):
        return {"row": x, "col": value * 4 + y, "depth": d}

    def at_y(value):
        return {"row": x, "col": z * 4 + value, "depth": d}

    sibling = {"row": x, "col": c, "depth": 1 - d}

    def remote(src, dst, send, recv, device):
        return pltpu.make_async_remote_copy(
            src_ref=src, dst_ref=dst, send_sem=send, recv_sem=recv, device_id=device, device_id_type=MESH
        )

    sent = []

    def push(src, dst, send, recv, device):
        copy = remote(src, dst, send, recv, device)
        copy.start()
        sent.append(copy)

    def arrived(ref, send, recv):
        remote(ref, ref, send, recv, sibling).wait_recv()

    load_tok = pltpu.make_async_copy(tokens, slabs.at[FWD, z, y], load_sem.at[0])
    load_cot = pltpu.make_async_copy(cotangent, slabs.at[BWD, z, y], load_sem.at[1])
    load_in = pltpu.make_async_copy(w_in_hbm, w_in, load_sem.at[2])
    load_out = pltpu.make_async_copy(w_out_hbm, w_out, load_sem.at[3])
    for load in (load_tok, load_cot, load_in, load_out):
        load.start()

    barrier = pltpu.get_barrier_semaphore()
    peers = [at_x(left), at_x(right), sibling]
    for step in (1, 3):
        peers += [at_z(mod4(z + step)), at_y(mod4(y + step))]
    for peer in peers:
        pl.semaphore_signal(barrier, inc=1, device_id=peer, device_id_type=MESH)
    pl.semaphore_wait(barrier, len(peers))

    def place(direction, k):
        return mod4(axis_me[direction] + STEP[k])

    def chunk(ref, direction, at):
        return ref.at[at] if direction == FWD else ref.at[:, at]

    def near(direction, value):
        return at_y(value) if direction == FWD else at_z(value)

    def far(direction, value):
        return at_z(value) if direction == FWD else at_y(value)

    def near_me(direction):
        return axis_me[1 - direction]

    def far_me(direction):
        return axis_me[direction]

    low_rows, high_rows = pl.ds(0, 16), pl.ds(16, 16)
    low_blocks, high_blocks = pl.ds(0, 2), pl.ds(2, 2)

    class Spread:
        def __init__(self, item, me, to, halves, send, recv):
            self.item, self.me, self.to, self.halves = item, me, to, halves
            self.send, self.recv = send, recv

        def part(self, offset, half):
            return self.item(mod4(self.me + offset)).at[self.halves[half]]

        def start(self):
            own, to = self.item(self.me), self.to
            for half, n, step in ((0, 0, 1), (1, 1, -1), (1, 2, 1), (0, 3, -1)):
                part = own.at[self.halves[half]]
                push(part, part, self.send(n), self.recv(n), to(mod4(self.me + step)))

        def mid(self):
            for half, n, source, step in ((0, 0, -1, 1), (1, 1, 1, -1)):
                part = self.part(source, half)
                arrived(part, self.send(n), self.recv(n))
                push(part, part, self.send(n + 4), self.recv(n + 4), self.to(mod4(self.me + step)))

        def neighbour(self, step):
            if step == 1:
                arrived(self.part(1, 0), self.send(3), self.recv(3))
            else:
                arrived(self.part(-1, 1), self.send(2), self.recv(2))

        def end(self):
            arrived(self.part(2, 0), self.send(4), self.recv(4))
            arrived(self.part(2, 1), self.send(5), self.recv(5))

    class Scatter:
        def __init__(self, piece, me, to, halves, passing, final, send, recv, add):
            self.piece, self.me, self.to, self.halves = piece, me, to, halves
            self.passing, self.final, self.send, self.recv, self.add = passing, final, send, recv, add

        def start_far(self):
            piece = self.piece(mod4(self.me + 2))
            for half, step in ((0, 1), (1, -1)):
                push(piece.at[self.halves[half]], self.passing.at[half], self.send(half), self.recv(half),
                     self.to(mod4(self.me + step)))

        def start_near(self, step):
            side = 0 if step == 1 else 1
            half = self.halves[1 - side]
            push(self.piece(mod4(self.me + step)).at[half], self.final.at[side, half],
                 self.send(2 + side), self.recv(2 + side), self.to(mod4(self.me + step)))

        def mid(self, step):
            side = 0 if step == 1 else 1
            half = self.halves[side]
            arrived(self.passing.at[side], self.send(side), self.recv(side))
            mine = self.piece(mod4(self.me + step)).at[half]
            self.add(mine, self.passing.at[side])
            push(mine, self.final.at[side, half], self.send(4 + side), self.recv(4 + side),
                 self.to(mod4(self.me + step)))

        def end(self):
            for side in (0, 1):
                arrived(self.final.at[side, self.halves[1 - side]], self.send(2 + side), self.recv(2 + side))
            for side in (0, 1):
                arrived(self.final.at[side, self.halves[side]], self.send(4 + side), self.recv(4 + side))

    def add_rows(mine, more):
        mine[...] = (mine[...].astype(f32) + more[...].astype(f32)).astype(bf16)

    def add_blocks(mine, more):
        for i in range(2):
            add_rows(mine.at[i], more.at[i])

    def ring(ref, *where):
        return lambda n: ref.at[(*where, n)]

    gather_near, gather_far, col_far, col_near = [], [], [], []
    for direction in (FWD, BWD):
        def own_line(at, direction=direction):
            return chunk(slabs.at[direction], direction, far_me(direction)).at[at]

        def whole_chunk(at, direction=direction):
            return chunk(slabs.at[direction], direction, at)

        def near_to(value, direction=direction):
            return near(direction, value)

        def far_to(value, direction=direction):
            return far(direction, value)

        def partial_chunk(at, direction=direction):
            return share2.at[direction, at]

        def summed_block(at, direction=direction):
            return row_sum.at[direction, at]

        gather_near.append(Spread(own_line, near_me(direction), near_to, (low_rows, high_rows),
                                  ring(gather_s, direction, 0), ring(gather_r, direction, 0)))
        gather_far.append(Spread(whole_chunk, far_me(direction), far_to, (low_blocks, high_blocks),
                                 ring(gather_s, direction, 1), ring(gather_r, direction, 1)))
        col_far.append(Scatter(partial_chunk, far_me(direction), far_to, (low_blocks, high_blocks),
                               passing1.at[direction], final1.at[direction],
                               ring(col_s, direction, 0), ring(col_r, direction, 0), add_blocks))
        col_near.append(Scatter(summed_block, near_me(direction), near_to, (low_rows, high_rows),
                                passing2.at[direction], final2.at[direction],
                                ring(col_s, direction, 1), ring(col_r, direction, 1), add_rows))

    def block_of(direction, at, owner):
        block = mod4(owner - at)
        return act.at[direction, at, block] if direction == FWD else act.at[direction, block, at]

    x_sum, x_spread = [[], []], [[], []]
    for direction in (FWD, BWD):
        for k in range(4):
            def piece(owner, direction=direction, at=place(direction, k)):
                return share.at[direction, at, mod4(owner - at)]

            def item(owner, direction=direction, at=place(direction, k)):
                return block_of(direction, at, owner)

            x_sum[direction].append(Scatter(
                piece, x, at_x, (low_rows, high_rows), passing.at[direction, k], final.at[direction, k],
                ring(scat_s, direction, k), ring(scat_r, direction, k), add_rows))
            x_spread[direction].append(Spread(
                item, x, at_x, (low_rows, high_rows), ring(spread_s, direction, k), ring(spread_r, direction, k)))

    def to_sibling(direction, k):
        at = place(direction, k)
        push(chunk(slabs.at[direction], direction, at), chunk(other.at[direction], direction, at),
             depth_s.at[direction, k], depth_r.at[direction, k], sibling)

    def first_matmul(direction, k):
        at = place(direction, k)
        if k == 1:
            gather_far[direction].neighbour(1)
        elif k == 2:
            gather_far[direction].neighbour(-1)
        elif k == 3:
            gather_far[direction].end()
        lhs = chunk(slabs.at[direction], direction, at)
        if k:
            to_sibling(direction, k)

        def tile(i, carry):
            cols = pl.ds(pl.multiple_of(i * TILE, TILE), TILE)
            rows = lhs[...].reshape(128, 1536)
            if direction == FWD:
                product = jnp.dot(rows, w_in[:, cols], preferred_element_type=f32)
            else:
                product = lax.dot_general(rows, w_out[cols, :], contract_last, preferred_element_type=f32)
            share[direction, at, :, :, cols] = product.astype(bf16).reshape(4, 32, TILE)
            return carry

        lax.fori_loop(0, 1536 // TILE, tile, 0)
        scatter = x_sum[direction][k]
        scatter.start_far()
        scatter.start_near(1)
        scatter.start_near(-1)

    def pass_on(direction, k):
        x_sum[direction][k].mid(1)
        x_sum[direction][k].mid(-1)

    def activate(direction, k):
        at = place(direction, k)
        x_sum[direction][k].end()
        block = mod4(x - at)
        mine = share.at[direction, at, block]
        place_z = at if direction == FWD else block
        result = block_of(direction, at, x)

        def rows(i, carry):
            part = pl.ds(pl.multiple_of(i * 16, 16), 16)
            total = mine[part].astype(f32)
            total = total + final[direction, k, 0, part].astype(f32)
            total = total + final[direction, k, 1, part].astype(f32)
            if direction == FWD:
                pre[place_z, part] = total
                result[part] = gelu_value(total).astype(bf16)
            else:
                result[part] = (total * gelu_slope(pre[place_z, part])).astype(bf16)
            return carry

        lax.fori_loop(0, 2, rows, 0)
        x_spread[direction][k].start()

    def forward_on(direction, k):
        x_spread[direction][k].mid()

    def second_matmul(direction, k):
        at = place(direction, k)
        x_spread[direction][k].neighbour(1)
        x_spread[direction][k].neighbour(-1)
        x_spread[direction][k].end()
        lhs = chunk(act.at[direction], direction, at)
        half = pl.ds(pl.multiple_of((1 - d) * 768, 128), 768)
        push(lhs.at[:, :, half], chunk(act_other.at[direction], direction, at),
             depth_s.at[direction, 4 + k], depth_r.at[direction, 4 + k], sibling)

        def tile(i, carry):
            cols = pl.ds(pl.multiple_of(i * TILE, TILE), TILE)
            rows = lhs[...].reshape(128, 1536)
            if direction == FWD:
                product = jnp.dot(rows, w_out[:, cols], preferred_element_type=f32)
            else:
                product = lax.dot_general(rows, w_in[cols, :], contract_last, preferred_element_type=f32)
            share2[direction, at, :, :, cols] = product.astype(bf16).reshape(4, 32, TILE)
            return carry

        lax.fori_loop(0, 1536 // TILE, tile, 0)
        scatter = col_far[direction]
        if k == 3:
            scatter.start_far()
        elif k:
            scatter.start_near(1 if k == 1 else -1)

    def far_mid(direction, step):
        col_far[direction].mid(step)

    def sum_far(direction):
        col_far[direction].end()
        at = place(direction, 0)

        def block(i, carry):
            total = share2[direction, at, i].astype(f32)
            for side in (0, 1):
                total = total + final1[direction, side, i].astype(f32)
            row_sum[direction, i] = total.astype(bf16)
            return carry

        lax.fori_loop(0, 4, block, 0)
        col_near[direction].start_far()
        col_near[direction].start_near(1)
        col_near[direction].start_near(-1)

    def near_mid(direction):
        col_near[direction].mid(1)
        col_near[direction].mid(-1)

    stores = []

    def sum_near(direction):
        col_near[direction].end()
        total = row_sum[direction, near_me(direction)].astype(f32)
        for side in (0, 1):
            total = total + final2[direction, side].astype(f32)
        out_buf[direction] = total.astype(bf16)
        store = pltpu.make_async_copy(out_buf.at[direction], (output, grad_tokens)[direction], store_sem.at[direction])
        store.start()
        stores.append(store)

    def grad_ready(which):
        for k in range(4):
            arrived(chunk(other.at[1 - which], 1 - which, place(1 - which, k)),
                    depth_s.at[1 - which, k], depth_r.at[1 - which, k])
            arrived(chunk(act_other.at[which], which, place(which, k)),
                    depth_s.at[which, 4 + k], depth_r.at[which, 4 + k])

    def weight_grad(which, first, last):
        width = 768 if which == FWD else 1536
        half = pl.multiple_of(d * 768, 128)
        result = gw_out if which == FWD else gw_in
        target = grad_w_out if which == FWD else grad_w_in

        def tile(i, carry):
            start = pl.multiple_of(i * 256, 256)
            rows = pl.ds(start, 256)
            if which == FWD:
                lhs = act[FWD, :, :, :, pl.ds(half + start, 256)].reshape(512, 256)
                rhs = slabs[BWD].reshape(512, 1536)
                lhs_other = act_other[FWD, :, :, :, rows].reshape(512, 256)
                rhs_other = other[BWD].reshape(512, 1536)
            else:
                lhs = slabs[FWD, :, :, :, rows].reshape(512, 256)
                rhs = act[BWD, :, :, :, pl.ds(half, 768)].reshape(512, 768)
                lhs_other = other[FWD, :, :, :, rows].reshape(512, 256)
                rhs_other = act_other[BWD].reshape(512, 768)
            product = lax.dot_general(lhs, rhs, contract_first, preferred_element_type=f32)
            product = product + lax.dot_general(lhs_other, rhs_other, contract_first, preferred_element_type=f32)
            result[rows] = product.astype(bf16)
            return carry

        lax.fori_loop(first, last, tile, 0)
        if last == width // 256:
            store = pltpu.make_async_copy(result, target, store_sem.at[2 + which])
            store.start()
            stores.append(store)

    F, B = FWD, BWD
    load_tok.wait()
    gather_near[F].start()
    load_cot.wait()
    gather_near[B].start()
    gather_near[F].mid()
    gather_near[B].mid()
    gather_near[F].neighbour(1)
    gather_near[F].neighbour(-1)
    gather_near[F].end()
    gather_far[F].start()
    to_sibling(F, 0)
    gather_near[B].neighbour(1)
    gather_near[B].neighbour(-1)
    gather_near[B].end()
    gather_far[B].start()
    to_sibling(B, 0)
    load_in.wait()
    first_matmul(F, 0)
    load_out.wait()
    first_matmul(B, 0)
    pass_on(F, 0)
    pass_on(B, 0)
    gather_far[F].mid()
    activate(F, 0)
    first_matmul(F, 1)
    first_matmul(F, 2)
    gather_far[B].mid()
    first_matmul(F, 3)
    forward_on(F, 0)
    pass_on(F, 3)
    pass_on(F, 1)
    pass_on(F, 2)
    first_matmul(B, 3)
    activate(F, 3)
    activate(F, 1)
    activate(F, 2)
    pass_on(B, 3)
    first_matmul(B, 1)
    second_matmul(F, 0)
    forward_on(F, 3)
    pass_on(B, 1)
    forward_on(F, 1)
    forward_on(F, 2)
    first_matmul(B, 2)
    second_matmul(F, 3)
    activate(B, 1)
    activate(B, 3)
    second_matmul(F, 1)
    second_matmul(F, 2)
    pass_on(B, 2)
    grad_ready(F)
    weight_grad(F, 0, 1)
    forward_on(B, 3)
    far_mid(F, 1)
    forward_on(B, 1)
    far_mid(F, -1)
    activate(B, 2)
    second_matmul(B, 3)
    forward_on(B, 2)
    second_matmul(B, 1)
    second_matmul(B, 2)
    activate(B, 0)
    far_mid(B, 1)
    weight_grad(F, 1, 2)
    far_mid(B, -1)
    forward_on(B, 0)
    weight_grad(F, 2, 3)
    second_matmul(B, 0)
    grad_ready(B)
    weight_grad(B, 0, 1)
    sum_far(F)
    sum_far(B)
    weight_grad(B, 1, 4)
    near_mid(F)
    near_mid(B)
    weight_grad(B, 4, 6)
    sum_near(F)
    sum_near(B)
    for copy in sent:
        copy.wait_send()
    for store in stores:
        store.wait()


def hand_on(*refs):
    for source, target in zip(refs[:4], refs[4:]):
        target[...] = source[...]


def body(tokens, w_in, w_out, cotangent):
    anywhere = pl.BlockSpec(memory_space=pl.ANY)
    dma = pltpu.SemaphoreType.DMA
    vmem = pltpu.VMEM
    results = pl.pallas_call(
        kernel,
        out_shape=(
            jax.ShapeDtypeStruct((32, 1536), bf16),
            jax.ShapeDtypeStruct((32, 1536), bf16),
            jax.ShapeDtypeStruct((1536, 768), bf16),
            jax.ShapeDtypeStruct((768, 1536), bf16),
        ),
        in_specs=[anywhere] * 4,
        out_specs=(anywhere,) * 4,
        scratch_shapes=[
            vmem((1536, 1536), bf16),
            vmem((1536, 1536), bf16),
            vmem((2, 4, 4, 32, 1536), bf16),
            vmem((2, 4, 4, 32, 1536), bf16),
            vmem((2, 4, 4, 32, 1536), bf16),
            vmem((2, 4, 2, 16, 1536), bf16),
            vmem((2, 4, 2, 32, 1536), bf16),
            vmem((4, 32, 1536), f32),
            vmem((2, 4, 4, 32, 1536), bf16),
            vmem((2, 4, 4, 32, 768), bf16),
            vmem((2, 4, 4, 32, 1536), bf16),
            vmem((2, 2, 2, 32, 1536), bf16),
            vmem((2, 2, 4, 32, 1536), bf16),
            vmem((2, 4, 32, 1536), bf16),
            vmem((2, 2, 16, 1536), bf16),
            vmem((2, 2, 32, 1536), bf16),
            vmem((2, 32, 1536), bf16),
            vmem((1536, 768), bf16),
            vmem((768, 1536), bf16),
            dma((4,)),
            dma((2, 2, 6)), dma((2, 2, 6)),
            dma((2, 4, 6)), dma((2, 4, 6)),
            dma((2, 4, 6)), dma((2, 4, 6)),
            dma((2, 8)), dma((2, 8)),
            dma((2, 2, 6)), dma((2, 2, 6)),
            dma((4,)),
        ],
        compiler_params=pltpu.CompilerParams(
            collective_id=1, has_side_effects=True, vmem_limit_bytes=60 * 2**20
        ),
        cost_estimate=pl.CostEstimate(flops=14_500_000_000, bytes_accessed=15_000_000, transcendentals=0),
        name="ffn_block",
    )(tokens, w_in, w_out, cotangent)
    blocks = [pl.BlockSpec((r.shape[0] // 2, r.shape[1]), lambda i: (i, 0)) for r in results]
    return pl.pallas_call(
        hand_on,
        grid=(2,),
        out_shape=tuple(jax.ShapeDtypeStruct(r.shape, r.dtype) for r in results),
        in_specs=blocks,
        out_specs=tuple(blocks),
        name="hand_on",
    )(*results)


def solution(mesh):
    in_specs = (
        P(("depth", "col"), "row"),
        P("row", "col"),
        P("col", "row"),
        P(("depth", "col"), "row"),
    )
    out_specs = (
        P(("depth", "col"), "row"),
        P(("depth", "col"), "row"),
        P("row", ("col", "depth")),
        P(("col", "depth"), "row"),
    )
    return jax.shard_map(body, mesh=mesh, in_specs=in_specs, out_specs=out_specs, check_vma=False)
```

time: 105 us -> 96.3 us (0.917)
  local copies, waits for them, and re-layouts: 7.86 us -> 0 us
    unnamed x6 -> x0, local copies, waits for them, and re-layouts: 7.86 us -> none
    pallas_call x1, Pallas kernels: 96.5 us -> 91.4 us  [body(): pl.pallas_call(kernel, out_shape=(jax.ShapeDtypeStruct((32, 1536), bf16),...]
    pallas_call x0 -> x1, Pallas kernels: none -> 4.11 us  [body(): pl.pallas_call(hand_on, grid=(2,), out_shape=tuple((jax.ShapeDtypeStruct(...]
where the time goes in v2:
time: 96.3 us; the launch traced here: 96.2 us
  Pallas kernels  95.5 us (99%)
    pallas_call x1, Pallas kernels, body(): pl.pallas_call(kernel, out_shape=(jax.ShapeDtypeStruct((32, 1536), bf16),...  91.4 us
    pallas_call x1, Pallas kernels, body(): pl.pallas_call(hand_on, grid=(2,), out_shape=tuple((jax.ShapeDtypeStruct(...  4.11 us

profile of v2, /device:TPU:0, one launch (start us, length us, event | category | flops | bytes accessed | tf_op | source)
XLA Modules:
  0.0 96.2 jit_solution(12846784773331365956)
XLA Ops:
  0.6 91.4 %ffn_block.1 = (bf16[32,1536]{1,0:T(8,128)(2,1)}, bf16[32,1536]{1,0:T(8,128)(2,1)}, bf16[1536,768]{1,0:T(8,128)(2,1)}, bf16[768,1536]{1,0:T(8,128)(2,1)}) custom-call(bf16[32,1536]{1,0:T(8,128)(2,1)} %tokens.1, bf16[1536,1536]{1,0:T(8,128)(2,1)} %w_in_hbm.1, bf16[1536,1536]{1,0:T(8,128)(2,1)} %w_out_hbm.1, bf16[32,1536]{1,0:T(8,128)(2,1)} %cotangent.1), custom_call_target="tpu_custom_call" | custom-call | flops 14499999744 | bytes 15000000 | tf_op jit(solution)/shard_map/ffn_block/pallas_call | solution.py:492
  92.0 4.1 %hand_on.1 = (bf16[32,1536]{1,0:T(8,128)(2,1)}, bf16[32,1536]{1,0:T(8,128)(2,1)}, bf16[1536,768]{1,0:T(8,128)(2,1)}, bf16[768,1536]{1,0:T(8,128)(2,1)}) custom-call(bf16[32,1536]{1,0:T(8,128)(2,1)} %get-tuple-element.8.refs_0_, bf16[32,1536]{1,0:T(8,128)(2,1)} %get-tuple-element.9.refs_1_, bf16[1536,768]{1,0:T(8,128)(2,1)} %get-tuple-element.10.refs_2_, ...), custom_call_target="tpu_custom_call" | custom-call | tf_op jit(solution)/shard_map/hand_on/pallas_call | solution.py:537

commit v3 on v2

--- a/solution.py
+++ b/solution.py
@@ -14,7 +14,7 @@
 bf16 = jnp.bfloat16
 FWD, BWD = 0, 1
 STEP = (0, 1, 3, 2)
-TILE = 512
+TILE = 768
 
 
 def gelu_value(pre_act):
@@ -115,6 +115,12 @@
         def __init__(self, item, me, to, halves, send, recv):
             self.item, self.me, self.to, self.halves = item, me, to, halves
             self.send, self.recv = send, recv
+            self.here = set()
+
+        def need(self, n, offset, half):
+            if n not in self.here:
+                self.here.add(n)
+                arrived(self.part(offset, half), self.send(n), self.recv(n))
 
         def part(self, offset, half):
             return self.item(mod4(self.me + offset)).at[self.halves[half]]
@@ -127,19 +133,17 @@
 
         def mid(self):
             for half, n, source, step in ((0, 0, -1, 1), (1, 1, 1, -1)):
+                self.need(n, source, half)
                 part = self.part(source, half)
-                arrived(part, self.send(n), self.recv(n))
                 push(part, part, self.send(n + 4), self.recv(n + 4), self.to(mod4(self.me + step)))
 
         def neighbour(self, step):
-            if step == 1:
-                arrived(self.part(1, 0), self.send(3), self.recv(3))
-            else:
-                arrived(self.part(-1, 1), self.send(2), self.recv(2))
+            for n, half in ((1, 1), (3, 0)) if step == 1 else ((0, 0), (2, 1)):
+                self.need(n, step, half)
 
         def end(self):
-            arrived(self.part(2, 0), self.send(4), self.recv(4))
-            arrived(self.part(2, 1), self.send(5), self.recv(5))
+            self.need(4, 2, 0)
+            self.need(5, 2, 1)
 
     class Scatter:
         def __init__(self, piece, me, to, halves, passing, final, send, recv, add):
@@ -188,9 +192,6 @@
         def own_line(at, direction=direction):
             return chunk(slabs.at[direction], direction, far_me(direction)).at[at]
 
-        def whole_chunk(at, direction=direction):
-            return chunk(slabs.at[direction], direction, at)
-
         def near_to(value, direction=direction):
             return near(direction, value)
 
@@ -205,8 +206,14 @@
 
         gather_near.append(Spread(own_line, near_me(direction), near_to, (low_rows, high_rows),
                                   ring(gather_s, direction, 0), ring(gather_r, direction, 0)))
-        gather_far.append(Spread(whole_chunk, far_me(direction), far_to, (low_blocks, high_blocks),
-                                 ring(gather_s, direction, 1), ring(gather_r, direction, 1)))
+        lines = []
+        for j in range(4):
+            def far_line(at, direction=direction, block=mod4(near_me(direction) + STEP[j])):
+                return chunk(slabs.at[direction], direction, at).at[block]
+
+            lines.append(Spread(far_line, far_me(direction), far_to, (low_rows, high_rows),
+                                ring(gather_s, direction, 1 + j), ring(gather_r, direction, 1 + j)))
+        gather_far.append(lines)
         col_far.append(Scatter(partial_chunk, far_me(direction), far_to, (low_blocks, high_blocks),
                                passing1.at[direction], final1.at[direction],
                                ring(col_s, direction, 0), ring(col_r, direction, 0), add_blocks))
@@ -240,12 +247,13 @@
 
     def first_matmul(direction, k):
         at = place(direction, k)
-        if k == 1:
-            gather_far[direction].neighbour(1)
-        elif k == 2:
-            gather_far[direction].neighbour(-1)
-        elif k == 3:
-            gather_far[direction].end()
+        for line in gather_far[direction]:
+            if k == 1:
+                line.neighbour(1)
+            elif k == 2:
+                line.neighbour(-1)
+            elif k == 3:
+                line.end()
         lhs = chunk(slabs.at[direction], direction, at)
         if k:
             to_sibling(direction, k)
@@ -301,6 +309,8 @@
         x_spread[direction][k].neighbour(1)
         x_spread[direction][k].neighbour(-1)
         x_spread[direction][k].end()
+        if k == 0 and direction == BWD:
+            col_far[direction].end()
         lhs = chunk(act.at[direction], direction, at)
         half = pl.ds(pl.multiple_of((1 - d) * 768, 128), 768)
         push(lhs.at[:, :, half], chunk(act_other.at[direction], direction, at),
@@ -313,6 +323,12 @@
                 product = jnp.dot(rows, w_out[:, cols], preferred_element_type=f32)
             else:
                 product = lax.dot_general(rows, w_in[cols, :], contract_last, preferred_element_type=f32)
+            if k == 0 and direction == BWD:
+                product = product.reshape(4, 32, TILE)
+                for side in (0, 1):
+                    product = product + final1[direction, side, :, :, cols].astype(f32)
+                row_sum[direction, :, :, cols] = product.astype(bf16)
+                return carry
             share2[direction, at, :, :, cols] = product.astype(bf16).reshape(4, 32, TILE)
             return carry
 
@@ -327,7 +343,6 @@
         col_far[direction].mid(step)
 
     def sum_far(direction):
-        col_far[direction].end()
         at = place(direction, 0)
 
         def block(i, carry):
@@ -337,7 +352,9 @@
             row_sum[direction, i] = total.astype(bf16)
             return carry
 
-        lax.fori_loop(0, 4, block, 0)
+        if direction == FWD:
+            col_far[direction].end()
+            lax.fori_loop(0, 4, block, 0)
         col_near[direction].start_far()
         col_near[direction].start_near(1)
         col_near[direction].start_near(-1)
@@ -400,80 +417,93 @@
     gather_near[F].start()
     load_cot.wait()
     gather_near[B].start()
+    gather_far[B][0].start()
+    gather_far[F][0].start()
+    gather_near[B].mid()
     gather_near[F].mid()
-    gather_near[B].mid()
+    gather_near[B].neighbour(1)
+    gather_near[B].neighbour(-1)
     gather_near[F].neighbour(1)
     gather_near[F].neighbour(-1)
+    gather_far[F][1].start()
+    gather_far[F][2].start()
+    gather_far[B][1].start()
+    gather_far[B][2].start()
     gather_near[F].end()
-    gather_far[F].start()
     to_sibling(F, 0)
-    gather_near[B].neighbour(1)
-    gather_near[B].neighbour(-1)
     gather_near[B].end()
-    gather_far[B].start()
     to_sibling(B, 0)
     load_in.wait()
     first_matmul(F, 0)
+    gather_far[B][3].start()
+    gather_far[F][3].start()
     load_out.wait()
     first_matmul(B, 0)
+    gather_far[B][2].mid()
+    gather_far[F][0].mid()
+    gather_far[B][0].mid()
+    gather_far[F][1].mid()
+    gather_far[F][2].mid()
     pass_on(F, 0)
+    gather_far[B][3].mid()
+    gather_far[F][3].mid()
+    gather_far[B][1].mid()
+    first_matmul(F, 1)
+    first_matmul(B, 1)
+    first_matmul(F, 3)
+    first_matmul(F, 2)
+    first_matmul(B, 2)
+    pass_on(B, 1)
+    pass_on(F, 1)
+    pass_on(F, 3)
+    pass_on(F, 2)
+    pass_on(B, 2)
+    first_matmul(B, 3)
+    activate(F, 1)
+    pass_on(B, 3)
+    activate(F, 0)
+    activate(F, 3)
+    activate(F, 2)
+    activate(B, 3)
+    activate(B, 1)
+    forward_on(B, 3)
+    forward_on(F, 3)
+    activate(B, 2)
+    forward_on(B, 1)
+    second_matmul(B, 3)
+    forward_on(B, 2)
     pass_on(B, 0)
-    gather_far[F].mid()
-    activate(F, 0)
-    first_matmul(F, 1)
-    first_matmul(F, 2)
-    gather_far[B].mid()
-    first_matmul(F, 3)
-    forward_on(F, 0)
-    pass_on(F, 3)
-    pass_on(F, 1)
-    pass_on(F, 2)
-    first_matmul(B, 3)
-    activate(F, 3)
-    activate(F, 1)
-    activate(F, 2)
-    pass_on(B, 3)
-    first_matmul(B, 1)
-    second_matmul(F, 0)
-    forward_on(F, 3)
-    pass_on(B, 1)
     forward_on(F, 1)
     forward_on(F, 2)
-    first_matmul(B, 2)
     second_matmul(F, 3)
-    activate(B, 1)
-    activate(B, 3)
+    second_matmul(B, 1)
+    second_matmul(B, 2)
+    forward_on(F, 0)
+    activate(B, 0)
     second_matmul(F, 1)
     second_matmul(F, 2)
-    pass_on(B, 2)
+    far_mid(B, -1)
+    far_mid(F, -1)
+    far_mid(F, 1)
+    far_mid(B, 1)
+    forward_on(B, 0)
+    second_matmul(F, 0)
     grad_ready(F)
-    weight_grad(F, 0, 1)
-    forward_on(B, 3)
-    far_mid(F, 1)
-    forward_on(B, 1)
-    far_mid(F, -1)
-    activate(B, 2)
-    second_matmul(B, 3)
-    forward_on(B, 2)
-    second_matmul(B, 1)
-    second_matmul(B, 2)
-    activate(B, 0)
-    far_mid(B, 1)
-    weight_grad(F, 1, 2)
-    far_mid(B, -1)
-    forward_on(B, 0)
-    weight_grad(F, 2, 3)
+    weight_grad(F, 0, 2)
     second_matmul(B, 0)
+    sum_far(B)
     grad_ready(B)
     weight_grad(B, 0, 1)
     sum_far(F)
-    sum_far(B)
-    weight_grad(B, 1, 4)
+    weight_grad(B, 1, 3)
+    near_mid(B)
+    weight_grad(B, 3, 4)
     near_mid(F)
-    near_mid(B)
-    weight_grad(B, 4, 6)
+    weight_grad(B, 4, 5)
+    weight_grad(F, 2, 3)
+    sum_near(B)
+    weight_grad(B, 5, 6)
     sum_near(F)
-    sum_near(B)
     for copy in sent:
         copy.wait_send()
     for store in stores:
@@ -520,7 +550,7 @@
             vmem((1536, 768), bf16),
             vmem((768, 1536), bf16),
             dma((4,)),
-            dma((2, 2, 6)), dma((2, 2, 6)),
+            dma((2, 5, 6)), dma((2, 5, 6)),
             dma((2, 4, 6)), dma((2, 4, 6)),
             dma((2, 4, 6)), dma((2, 4, 6)),
             dma((2, 8)), dma((2, 8)),

time: 96.3 us -> 92.5 us (0.961)
  Pallas kernels: 95.5 us -> 91.8 us
    pallas_call x1, Pallas kernels: 91.4 us -> 87.7 us  [body(): pl.pallas_call(kernel, out_shape=(jax.ShapeDtypeStruct((32, 1536), bf16),...]
where the time goes in v3:
time: 92.5 us; the launch traced here: 92.4 us
  Pallas kernels  91.8 us (99%)
    pallas_call x1, Pallas kernels, body(): pl.pallas_call(kernel, out_shape=(jax.ShapeDtypeStruct((32, 1536), bf16),...  87.7 us
    pallas_call x1, Pallas kernels, body(): pl.pallas_call(hand_on, grid=(2,), out_shape=tuple((jax.ShapeDtypeStruct(...  4.11 us

profile of v3, /device:TPU:0, one launch (start us, length us, event | category | flops | bytes accessed | tf_op | source)
XLA Modules:
  0.0 92.4 jit_solution(5323005378764505617)
XLA Ops:
  0.6 87.7 %ffn_block.1 = (bf16[32,1536]{1,0:T(8,128)(2,1)}, bf16[32,1536]{1,0:T(8,128)(2,1)}, bf16[1536,768]{1,0:T(8,128)(2,1)}, bf16[768,1536]{1,0:T(8,128)(2,1)}) custom-call(bf16[32,1536]{1,0:T(8,128)(2,1)} %tokens.1, bf16[1536,1536]{1,0:T(8,128)(2,1)} %w_in_hbm.1, bf16[1536,1536]{1,0:T(8,128)(2,1)} %w_out_hbm.1, bf16[32,1536]{1,0:T(8,128)(2,1)} %cotangent.1), custom_call_target="tpu_custom_call" | custom-call | flops 14499999744 | bytes 15000000 | tf_op jit(solution)/shard_map/ffn_block/pallas_call | solution.py:522
  88.3 4.1 %hand_on.1 = (bf16[32,1536]{1,0:T(8,128)(2,1)}, bf16[32,1536]{1,0:T(8,128)(2,1)}, bf16[1536,768]{1,0:T(8,128)(2,1)}, bf16[768,1536]{1,0:T(8,128)(2,1)}) custom-call(bf16[32,1536]{1,0:T(8,128)(2,1)} %get-tuple-element.8.refs_0_, bf16[32,1536]{1,0:T(8,128)(2,1)} %get-tuple-element.9.refs_1_, bf16[1536,768]{1,0:T(8,128)(2,1)} %get-tuple-element.10.refs_2_, ...), custom_call_target="tpu_custom_call" | custom-call | tf_op jit(solution)/shard_map/hand_on/pallas_call | solution.py:567

commit v4 on v3

--- a/solution.py
+++ b/solution.py
@@ -8,7 +8,6 @@
 MESH = pl.DeviceIdType.MESH
 root_coeff = 0.7978845608028654
 cubic_coeff = 0.044715
-contract_last = (((1,), (1,)), ((), ()))
 contract_first = (((0,), (0,)), ((), ()))
 f32 = jnp.float32
 bf16 = jnp.bfloat16
@@ -37,10 +36,10 @@
 def kernel(
     tokens, w_in_hbm, w_out_hbm, cotangent,
     output, grad_tokens, grad_w_in, grad_w_out,
-    w_in, w_out, slabs, other, share, passing, final, pre, act, act_other,
+    w_in, w_out, w_in_t, w_out_t, slabs, other, share, passing, final, pre, act, act_other,
     share2, passing1, final1, row_sum, passing2, final2, out_buf, gw_in, gw_out,
     load_sem, gather_s, gather_r, scat_s, scat_r, spread_s, spread_r,
-    depth_s, depth_r, col_s, col_r, store_sem,
+    depth_s, depth_r, col_s, col_r, store_sem, grad_sem,
 ):
     x = lax.axis_index("row")
     c = lax.axis_index("col")
@@ -84,7 +83,7 @@
 
     barrier = pltpu.get_barrier_semaphore()
     peers = [at_x(left), at_x(right), sibling]
-    for step in (1, 3):
+    for step in (1, 2, 3):
         peers += [at_z(mod4(z + step)), at_y(mod4(y + step))]
     for peer in peers:
         pl.semaphore_signal(barrier, inc=1, device_id=peer, device_id_type=MESH)
@@ -112,7 +111,8 @@
     low_blocks, high_blocks = pl.ds(0, 2), pl.ds(2, 2)
 
     class Spread:
-        def __init__(self, item, me, to, halves, send, recv):
+        def __init__(self, item, me, to, halves, send, recv, direct=False):
+            self.direct = direct
             self.item, self.me, self.to, self.halves = item, me, to, halves
             self.send, self.recv = send, recv
             self.here = set()
@@ -130,8 +130,14 @@
             for half, n, step in ((0, 0, 1), (1, 1, -1), (1, 2, 1), (0, 3, -1)):
                 part = own.at[self.halves[half]]
                 push(part, part, self.send(n), self.recv(n), to(mod4(self.me + step)))
+            if self.direct:
+                for half in (0, 1):
+                    part = own.at[self.halves[half]]
+                    push(part, part, self.send(4 + half), self.recv(4 + half), to(mod4(self.me + 2)))
 
         def mid(self):
+            if self.direct:
+                return
             for half, n, source, step in ((0, 0, -1, 1), (1, 1, 1, -1)):
                 self.need(n, source, half)
                 part = self.part(source, half)
@@ -146,7 +152,8 @@
             self.need(5, 2, 1)
 
     class Scatter:
-        def __init__(self, piece, me, to, halves, passing, final, send, recv, add):
+        def __init__(self, piece, me, to, halves, passing, final, send, recv, add, direct=False):
+            self.direct = direct
             self.piece, self.me, self.to, self.halves = piece, me, to, halves
             self.passing, self.final, self.send, self.recv, self.add = passing, final, send, recv, add
 
@@ -154,15 +161,21 @@
             piece = self.piece(mod4(self.me + 2))
             for half, step in ((0, 1), (1, -1)):
                 push(piece.at[self.halves[half]], self.passing.at[half], self.send(half), self.recv(half),
-                     self.to(mod4(self.me + step)))
+                     self.to(mod4(self.me + (2 if self.direct else step))))
 
         def start_near(self, step):
             side = 0 if step == 1 else 1
             half = self.halves[1 - side]
             push(self.piece(mod4(self.me + step)).at[half], self.final.at[side, half],
                  self.send(2 + side), self.recv(2 + side), self.to(mod4(self.me + step)))
+            if self.direct:
+                half = self.halves[side]
+                push(self.piece(mod4(self.me + step)).at[half], self.final.at[side, half],
+                     self.send(4 + side), self.recv(4 + side), self.to(mod4(self.me + step)))
 
         def mid(self, step):
+            if self.direct:
+                return
             side = 0 if step == 1 else 1
             half = self.halves[side]
             arrived(self.passing.at[side], self.send(side), self.recv(side))
@@ -172,6 +185,9 @@
                  self.to(mod4(self.me + step)))
 
         def end(self):
+            if self.direct:
+                for half in (0, 1):
+                    arrived(self.passing.at[half], self.send(half), self.recv(half))
             for side in (0, 1):
                 arrived(self.final.at[side, self.halves[1 - side]], self.send(2 + side), self.recv(2 + side))
             for side in (0, 1):
@@ -201,11 +217,8 @@
         def partial_chunk(at, direction=direction):
             return share2.at[direction, at]
 
-        def summed_block(at, direction=direction):
-            return row_sum.at[direction, at]
-
         gather_near.append(Spread(own_line, near_me(direction), near_to, (low_rows, high_rows),
-                                  ring(gather_s, direction, 0), ring(gather_r, direction, 0)))
+                                  ring(gather_s, direction, 0), ring(gather_r, direction, 0), True))
         lines = []
         for j in range(4):
             def far_line(at, direction=direction, block=mod4(near_me(direction) + STEP[j])):
@@ -217,9 +230,15 @@
         col_far.append(Scatter(partial_chunk, far_me(direction), far_to, (low_blocks, high_blocks),
                                passing1.at[direction], final1.at[direction],
                                ring(col_s, direction, 0), ring(col_r, direction, 0), add_blocks))
-        col_near.append(Scatter(summed_block, near_me(direction), near_to, (low_rows, high_rows),
-                                passing2.at[direction], final2.at[direction],
-                                ring(col_s, direction, 1), ring(col_r, direction, 1), add_rows))
+        halves = []
+        for h in (0, 1):
+            def summed_block(at, direction=direction, h=h):
+                return row_sum.at[direction, h, at]
+
+            halves.append(Scatter(summed_block, near_me(direction), near_to, (low_rows, high_rows),
+                                  passing2.at[direction, h], final2.at[direction, h],
+                                  ring(col_s, direction, 1 + h), ring(col_r, direction, 1 + h), add_rows, True))
+        col_near.append(halves)
 
     def block_of(direction, at, owner):
         block = mod4(owner - at)
@@ -239,6 +258,15 @@
                 ring(scat_s, direction, k), ring(scat_r, direction, k), add_rows))
             x_spread[direction].append(Spread(
                 item, x, at_x, (low_rows, high_rows), ring(spread_s, direction, k), ring(spread_r, direction, k)))
+
+    def turn(direction, i):
+        rows = pl.ds(i * 512, 512)
+        if direction == FWD:
+            w_in_t[:, rows] = w_in[rows, :].T
+        else:
+            w_out_t[:, rows] = w_out[rows, :].T
+
+    far_mids, at_once = [0, 0], [False, False]
 
     def to_sibling(direction, k):
         at = place(direction, k)
@@ -264,7 +292,7 @@
             if direction == FWD:
                 product = jnp.dot(rows, w_in[:, cols], preferred_element_type=f32)
             else:
-                product = lax.dot_general(rows, w_out[cols, :], contract_last, preferred_element_type=f32)
+                product = jnp.dot(rows, w_out_t[:, cols], preferred_element_type=f32)
             share[direction, at, :, :, cols] = product.astype(bf16).reshape(4, 32, TILE)
             return carry
 
@@ -309,8 +337,9 @@
         x_spread[direction][k].neighbour(1)
         x_spread[direction][k].neighbour(-1)
         x_spread[direction][k].end()
-        if k == 0 and direction == BWD:
+        if k == 0 and far_mids[direction] == 2:
             col_far[direction].end()
+            at_once[direction] = True
         lhs = chunk(act.at[direction], direction, at)
         half = pl.ds(pl.multiple_of((1 - d) * 768, 128), 768)
         push(lhs.at[:, :, half], chunk(act_other.at[direction], direction, at),
@@ -322,16 +351,21 @@
             if direction == FWD:
                 product = jnp.dot(rows, w_out[:, cols], preferred_element_type=f32)
             else:
-                product = lax.dot_general(rows, w_in[cols, :], contract_last, preferred_element_type=f32)
-            if k == 0 and direction == BWD:
+                product = jnp.dot(rows, w_in_t[:, cols], preferred_element_type=f32)
+            if k == 0 and at_once[direction]:
                 product = product.reshape(4, 32, TILE)
                 for side in (0, 1):
                     product = product + final1[direction, side, :, :, cols].astype(f32)
-                row_sum[direction, :, :, cols] = product.astype(bf16)
+                row_sum[direction, i] = product.astype(bf16)
                 return carry
             share2[direction, at, :, :, cols] = product.astype(bf16).reshape(4, 32, TILE)
             return carry
 
+        if k == 0 and at_once[direction]:
+            for h in (0, 1):
+                lax.fori_loop(h, h + 1, tile, 0)
+                near_start(direction, h)
+            return
         lax.fori_loop(0, 1536 // TILE, tile, 0)
         scatter = col_far[direction]
         if k == 3:
@@ -341,36 +375,45 @@
 
     def far_mid(direction, step):
         col_far[direction].mid(step)
+        far_mids[direction] += 1
+
+    def near_start(direction, h):
+        col_near[direction][h].start_far()
+        col_near[direction][h].start_near(1)
+        col_near[direction][h].start_near(-1)
 
     def sum_far(direction):
+        if at_once[direction]:
+            return
+        col_far[direction].end()
         at = place(direction, 0)
-
-        def block(i, carry):
-            total = share2[direction, at, i].astype(f32)
+        for h in (0, 1):
+            cols = pl.ds(h * TILE, TILE)
+
+            def block(i, carry):
+                total = share2[direction, at, i, :, cols].astype(f32)
+                for side in (0, 1):
+                    total = total + final1[direction, side, i, :, cols].astype(f32)
+                row_sum[direction, h, i] = total.astype(bf16)
+                return carry
+
+            lax.fori_loop(0, 4, block, 0)
+            near_start(direction, h)
+
+    def near_mid(direction, h):
+        col_near[direction][h].mid(1)
+        col_near[direction][h].mid(-1)
+
+    stores = []
+
+    def sum_near(direction):
+        for h in (0, 1):
+            col_near[direction][h].end()
+            total = row_sum[direction, h, near_me(direction)].astype(f32)
             for side in (0, 1):
-                total = total + final1[direction, side, i].astype(f32)
-            row_sum[direction, i] = total.astype(bf16)
-            return carry
-
-        if direction == FWD:
-            col_far[direction].end()
-            lax.fori_loop(0, 4, block, 0)
-        col_near[direction].start_far()
-        col_near[direction].start_near(1)
-        col_near[direction].start_near(-1)
-
-    def near_mid(direction):
-        col_near[direction].mid(1)
-        col_near[direction].mid(-1)
-
-    stores = []
-
-    def sum_near(direction):
-        col_near[direction].end()
-        total = row_sum[direction, near_me(direction)].astype(f32)
-        for side in (0, 1):
-            total = total + final2[direction, side].astype(f32)
-        out_buf[direction] = total.astype(bf16)
+                total = total + final2[direction, h, side].astype(f32)
+            total = total + passing2[direction, h].reshape(32, TILE).astype(f32)
+            out_buf[direction, :, pl.ds(h * TILE, TILE)] = total.astype(bf16)
         store = pltpu.make_async_copy(out_buf.at[direction], (output, grad_tokens)[direction], store_sem.at[direction])
         store.start()
         stores.append(store)
@@ -383,7 +426,6 @@
                     depth_s.at[which, 4 + k], depth_r.at[which, 4 + k])
 
     def weight_grad(which, first, last):
-        width = 768 if which == FWD else 1536
         half = pl.multiple_of(d * 768, 128)
         result = gw_out if which == FWD else gw_in
         target = grad_w_out if which == FWD else grad_w_in
@@ -407,102 +449,108 @@
             return carry
 
         lax.fori_loop(first, last, tile, 0)
-        if last == width // 256:
-            store = pltpu.make_async_copy(result, target, store_sem.at[2 + which])
-            store.start()
-            stores.append(store)
+        rows = pl.ds(first * 256, (last - first) * 256)
+        store = pltpu.make_async_copy(result.at[rows], target.at[rows], grad_sem.at[which, first])
+        store.start()
+        stores.append(store)
 
     F, B = FWD, BWD
     load_tok.wait()
     gather_near[F].start()
     load_cot.wait()
     gather_near[B].start()
+    load_out.wait()
+    turn(B, 2)
+    turn(B, 1)
+    load_in.wait()
+    turn(F, 1)
+    gather_far[F][0].start()
     gather_far[B][0].start()
-    gather_far[F][0].start()
-    gather_near[B].mid()
     gather_near[F].mid()
+    turn(B, 0)
     gather_near[B].neighbour(1)
     gather_near[B].neighbour(-1)
+    gather_near[B].mid()
+    gather_far[B][1].start()
+    gather_far[B][2].start()
     gather_near[F].neighbour(1)
     gather_near[F].neighbour(-1)
     gather_far[F][1].start()
     gather_far[F][2].start()
-    gather_far[B][1].start()
-    gather_far[B][2].start()
     gather_near[F].end()
     to_sibling(F, 0)
+    first_matmul(F, 0)
+    gather_far[F][3].start()
+    gather_far[F][0].mid()
     gather_near[B].end()
     to_sibling(B, 0)
-    load_in.wait()
-    first_matmul(F, 0)
     gather_far[B][3].start()
-    gather_far[F][3].start()
-    load_out.wait()
     first_matmul(B, 0)
-    gather_far[B][2].mid()
-    gather_far[F][0].mid()
-    gather_far[B][0].mid()
+    pass_on(F, 0)
+    first_matmul(B, 1)
     gather_far[F][1].mid()
+    first_matmul(F, 1)
     gather_far[F][2].mid()
-    pass_on(F, 0)
     gather_far[B][3].mid()
     gather_far[F][3].mid()
+    turn(F, 2)
+    turn(F, 0)
+    activate(F, 0)
+    first_matmul(F, 2)
+    gather_far[B][2].mid()
     gather_far[B][1].mid()
-    first_matmul(F, 1)
-    first_matmul(B, 1)
     first_matmul(F, 3)
-    first_matmul(F, 2)
+    gather_far[B][0].mid()
+    pass_on(F, 1)
+    first_matmul(B, 3)
+    pass_on(F, 2)
+    pass_on(B, 1)
+    activate(F, 1)
+    pass_on(F, 3)
+    pass_on(B, 3)
     first_matmul(B, 2)
-    pass_on(B, 1)
-    pass_on(F, 1)
-    pass_on(F, 3)
-    pass_on(F, 2)
+    activate(F, 2)
+    activate(F, 3)
+    activate(B, 3)
+    forward_on(F, 2)
     pass_on(B, 2)
-    first_matmul(B, 3)
-    activate(F, 1)
-    pass_on(B, 3)
-    activate(F, 0)
-    activate(F, 3)
-    activate(F, 2)
-    activate(B, 3)
+    forward_on(F, 3)
     activate(B, 1)
     forward_on(B, 3)
-    forward_on(F, 3)
     activate(B, 2)
     forward_on(B, 1)
+    second_matmul(F, 2)
+    forward_on(F, 1)
     second_matmul(B, 3)
     forward_on(B, 2)
+    second_matmul(F, 3)
     pass_on(B, 0)
-    forward_on(F, 1)
-    forward_on(F, 2)
-    second_matmul(F, 3)
     second_matmul(B, 1)
     second_matmul(B, 2)
     forward_on(F, 0)
+    second_matmul(F, 1)
     activate(B, 0)
-    second_matmul(F, 1)
-    second_matmul(F, 2)
+    far_mid(F, 1)
     far_mid(B, -1)
+    far_mid(B, 1)
+    second_matmul(F, 0)
     far_mid(F, -1)
-    far_mid(F, 1)
-    far_mid(B, 1)
     forward_on(B, 0)
-    second_matmul(F, 0)
     grad_ready(F)
     weight_grad(F, 0, 2)
     second_matmul(B, 0)
+    sum_far(F)
+    weight_grad(F, 2, 3)
+    grad_ready(B)
+    weight_grad(B, 0, 2)
     sum_far(B)
-    grad_ready(B)
-    weight_grad(B, 0, 1)
-    sum_far(F)
-    weight_grad(B, 1, 3)
-    near_mid(B)
-    weight_grad(B, 3, 4)
-    near_mid(F)
-    weight_grad(B, 4, 5)
-    weight_grad(F, 2, 3)
+    weight_grad(B, 2, 3)
+    near_mid(B, 0)
+    near_mid(F, 1)
+    near_mid(F, 0)
+    near_mid(B, 1)
+    weight_grad(B, 3, 6)
     sum_near(B)
-    weight_grad(B, 5, 6)
     sum_near(F)
     for copy in sent:
         copy.wait_send()
@@ -532,6 +580,8 @@
         scratch_shapes=[
             vmem((1536, 1536), bf16),
             vmem((1536, 1536), bf16),
+            vmem((1536, 1536), bf16),
+            vmem((1536, 1536), bf16),
             vmem((2, 4, 4, 32, 1536), bf16),
             vmem((2, 4, 4, 32, 1536), bf16),
             vmem((2, 4, 4, 32, 1536), bf16),
@@ -543,9 +593,9 @@
             vmem((2, 4, 4, 32, 1536), bf16),
             vmem((2, 2, 2, 32, 1536), bf16),
             vmem((2, 2, 4, 32, 1536), bf16),
-            vmem((2, 4, 32, 1536), bf16),
-            vmem((2, 2, 16, 1536), bf16),
-            vmem((2, 2, 32, 1536), bf16),
+            vmem((2, 2, 4, 32, 768), bf16),
+            vmem((2, 2, 2, 16, 768), bf16),
+            vmem((2, 2, 2, 32, 768), bf16),
             vmem((2, 32, 1536), bf16),
             vmem((1536, 768), bf16),
             vmem((768, 1536), bf16),
@@ -554,8 +604,9 @@
             dma((2, 4, 6)), dma((2, 4, 6)),
             dma((2, 4, 6)), dma((2, 4, 6)),
             dma((2, 8)), dma((2, 8)),
-            dma((2, 2, 6)), dma((2, 2, 6)),
-            dma((4,)),
+            dma((2, 3, 6)), dma((2, 3, 6)),
+            dma((2,)),
+            dma((2, 6)),
         ],
         compiler_params=pltpu.CompilerParams(
             collective_id=1, has_side_effects=True, vmem_limit_bytes=60 * 2**20
@@ -570,6 +621,7 @@
         out_shape=tuple(jax.ShapeDtypeStruct(r.shape, r.dtype) for r in results),
         in_specs=blocks,
         out_specs=tuple(blocks),
+        compiler_params=pltpu.CompilerParams(vmem_limit_bytes=60 * 2**20),
         name="hand_on",
     )(*results)
 

time: 92.5 us -> 91.2 us (0.986)
  Pallas kernels: 91.8 us -> 90.5 us
    pallas_call x1, Pallas kernels: 87.7 us -> 86.4 us  [body(): pl.pallas_call(kernel, out_shape=(jax.ShapeDtypeStruct((32, 1536), bf16),...]
where the time goes in v4:
time: 91.2 us; the launch traced here: 91.1 us
  Pallas kernels  90.5 us (99%)
    pallas_call x1, Pallas kernels, body(): pl.pallas_call(kernel, out_shape=(jax.ShapeDtypeStruct((32, 1536), bf16),...  86.4 us
    pallas_call x1, Pallas kernels, body(): pl.pallas_call(hand_on, grid=(2,), out_shape=tuple((jax.ShapeDtypeStruct(...  4.11 us

profile of v4, /device:TPU:0, one launch (start us, length us, event | category | flops | bytes accessed | tf_op | source)
XLA Modules:
  0.0 91.1 jit_solution(4138343951864268939)
XLA Ops:
  0.6 86.4 %ffn_block.1 = (bf16[32,1536]{1,0:T(8,128)(2,1)}, bf16[32,1536]{1,0:T(8,128)(2,1)}, bf16[1536,768]{1,0:T(8,128)(2,1)}, bf16[768,1536]{1,0:T(8,128)(2,1)}) custom-call(bf16[32,1536]{1,0:T(8,128)(2,1)} %tokens.1, bf16[1536,1536]{1,0:T(8,128)(2,1)} %w_in_hbm.1, bf16[1536,1536]{1,0:T(8,128)(2,1)} %w_out_hbm.1, bf16[32,1536]{1,0:T(8,128)(2,1)} %cotangent.1), custom_call_target="tpu_custom_call" | custom-call | flops 14499999744 | bytes 15000000 | tf_op jit(solution)/shard_map/ffn_block/pallas_call | solution.py:570
  87.0 4.1 %hand_on.1 = (bf16[32,1536]{1,0:T(8,128)(2,1)}, bf16[32,1536]{1,0:T(8,128)(2,1)}, bf16[1536,768]{1,0:T(8,128)(2,1)}, bf16[768,1536]{1,0:T(8,128)(2,1)}) custom-call(bf16[32,1536]{1,0:T(8,128)(2,1)} %get-tuple-element.8.refs_0_, bf16[32,1536]{1,0:T(8,128)(2,1)} %get-tuple-element.9.refs_1_, bf16[1536,768]{1,0:T(8,128)(2,1)} %get-tuple-element.10.refs_2_, ...), custom_call_target="tpu_custom_call" | custom-call | tf_op jit(solution)/shard_map/hand_on/pallas_call | solution.py:618

commit v5 on v4

--- a/solution.py
+++ b/solution.py
@@ -461,11 +461,11 @@
     gather_near[B].start()
     load_out.wait()
     turn(B, 2)
+    gather_far[B][0].start()
     turn(B, 1)
     load_in.wait()
     turn(F, 1)
     gather_far[F][0].start()
-    gather_far[B][0].start()
     gather_near[F].mid()
     turn(B, 0)
     gather_near[B].neighbour(1)
@@ -545,11 +545,12 @@
     weight_grad(B, 0, 2)
     sum_far(B)
     weight_grad(B, 2, 3)
-    near_mid(B, 0)
     near_mid(F, 1)
     near_mid(F, 0)
     near_mid(B, 1)
-    weight_grad(B, 3, 6)
+    weight_grad(B, 3, 4)
+    near_mid(B, 0)
+    weight_grad(B, 4, 6)
     sum_near(B)
     sum_near(F)
     for copy in sent:

time: 91.2 us -> 90.7 us (level)
  no operation moved by 1% of the time
where the time goes in v5:
time: 90.7 us; the launch traced here: 90.6 us
  Pallas kernels  89.9 us (99%)
    pallas_call x1, Pallas kernels, body(): pl.pallas_call(kernel, out_shape=(jax.ShapeDtypeStruct((32, 1536), bf16),...  85.8 us
    pallas_call x1, Pallas kernels, body(): pl.pallas_call(hand_on, grid=(2,), out_shape=tuple((jax.ShapeDtypeStruct(...  4.11 us

profile of v5, /device:TPU:0, one launch (start us, length us, event | category | flops | bytes accessed | tf_op | source)
XLA Modules:
  0.0 90.6 jit_solution(3306525960104638760)
XLA Ops:
  0.6 85.8 %ffn_block.1 = (bf16[32,1536]{1,0:T(8,128)(2,1)}, bf16[32,1536]{1,0:T(8,128)(2,1)}, bf16[1536,768]{1,0:T(8,128)(2,1)}, bf16[768,1536]{1,0:T(8,128)(2,1)}) custom-call(bf16[32,1536]{1,0:T(8,128)(2,1)} %tokens.1, bf16[1536,1536]{1,0:T(8,128)(2,1)} %w_in_hbm.1, bf16[1536,1536]{1,0:T(8,128)(2,1)} %w_out_hbm.1, bf16[32,1536]{1,0:T(8,128)(2,1)} %cotangent.1), custom_call_target="tpu_custom_call" | custom-call | flops 14499999744 | bytes 15000000 | tf_op jit(solution)/shard_map/ffn_block/pallas_call | solution.py:571
  86.5 4.1 %hand_on.1 = (bf16[32,1536]{1,0:T(8,128)(2,1)}, bf16[32,1536]{1,0:T(8,128)(2,1)}, bf16[1536,768]{1,0:T(8,128)(2,1)}, bf16[768,1536]{1,0:T(8,128)(2,1)}) custom-call(bf16[32,1536]{1,0:T(8,128)(2,1)} %get-tuple-element.8.refs_0_, bf16[32,1536]{1,0:T(8,128)(2,1)} %get-tuple-element.9.refs_1_, bf16[1536,768]{1,0:T(8,128)(2,1)} %get-tuple-element.10.refs_2_, ...), custom_call_target="tpu_custom_call" | custom-call | tf_op jit(solution)/shard_map/hand_on/pallas_call | solution.py:619
